TPU v7x, 32 devices: a whole 2x2x4 slice. The times are simulated.
32 devices in a mesh: row: 4 (over z), col: 8 (over y, x, core).
Axes of the slice: x: 2, y: 2, z: 4, core: 2. Of those that a mesh axis runs over, the one named last changes fastest.
Arguments:
- config: float32 [6, 4096], P(None, ('row', 'col')), as said below
- start: float32 [6, 4096], P(None, ('row', 'col')), may hold values from -6 to 6
- tile_list: int32 [4, 8, 8, 5], P('row', 'col'), may hold values from -1 to 7, as said below
- tile_count: int32 [4, 8], P('row', 'col'), may hold values from 1 to 8, as said below
Outputs:
- coefficients: float32 [4], replicated
- mode: float32 [6, 4096], P(None, ('row', 'col'))
Inputs may be any that keep to these rules, and one draw needn't show every extreme that they name: `tile_list`: entry k of device (r, c) is used when k < tile_count[r, c]; its first value is a row tile 0 to 7, its second a column tile 0 to 3, the last three are offsets in -1, 0, 1, not all zero. Unused entries hold values of the same law. `tile_count`: some device uses all 8 entries. `config`: rows 3 to 5 are unit vectors. No two ellipsoids intersect, within a tile or across tiles placed by a list entry's offsets.
All inputs are finite; a program needn't handle non-finite values.
Results may differ from a plain program's by a relative error of at most 0.0003.
Values sent between devices are 32-bit elements; how exact they have to be, the bound alone decides.
No kernel may reach another device: no remote copies, remote signals or barrier semaphores. Data moves between devices by JAX's collectives and lax.ppermute only.
A program may use at most 64 MiB of HBM per device.

v0:
```python
import functools
import math

import jax
import jax.numpy as jnp
from jax import lax
from jax.experimental import pallas as pl
from jax.experimental.pallas import tpu as pltpu
from jax.sharding import PartitionSpec as P

chi_shape = 0.8
chi_energy = (math.sqrt(5.0) - 1.0) / (math.sqrt(5.0) + 1.0)
well_depth = 0.005
cutoff_sq = 20.25
norm_eps = 1e-06

SUB = 8
LIST_ROW = 6
CODE_BITS = 6
GROUP = 2
TERMS = 20
HELD = 128
VMEM_LIMIT = 32 * 1024 * 1024


def dot3(a, b):
    return a[0] * b[0] + a[1] * b[1] + a[2] * b[2]


def cross3(a, b):
    return (
        a[1] * b[2] - a[2] * b[1],
        a[2] * b[0] - a[0] * b[2],
        a[0] * b[1] - a[1] * b[0],
    )


def bracket(chi, scaled, factor, p, a, b):
    f = factor * (a - scaled * b)
    g = factor * (b - scaled * a)
    y = p * (a * f + b * g)
    cross = factor * scaled
    f_c = chi * (cross * f - factor * g)
    g_c = chi * (cross * g - factor * f)
    return f, g, y, cross, f_c, g_c


def pair_coefficients(d, ui, uj, lift):
    r_sq = dot3(d, d) + lift
    a = dot3(d, ui)
    b = dot3(d, uj)
    c = dot3(ui, uj)
    r_inv = lax.rsqrt(r_sq)
    p = r_inv * r_inv
    p2 = 2.0 * p
    r = r_sq * r_inv
    x = jnp.maximum(1.0 - r_sq * (1.0 / cutoff_sq), 0.0)
    c_shape = chi_shape * c
    c_energy = chi_energy * c
    e1 = lax.rsqrt(1.0 - c_shape * c_shape)
    q = e1 * e1
    q2 = 1.0 / (1.0 - c_energy * c_energy)
    f, g, y, m, f_c, g_c = bracket(chi_shape, c_shape, q, p, a, b)
    f2, g2, y2, m2, f2_c, g2_c = bracket(chi_energy, c_energy, q2, p, a, b)
    sigma = lax.rsqrt(1.0 - chi_shape * y)
    sigma_sq = sigma * sigma
    psi = 1.0 - chi_energy * y2
    s = 1.0 / (r - sigma + 1.0)
    s_sq = s * s
    s6 = s_sq * s_sq * s_sq
    t0 = s6 * (s6 - 1.0)
    t1 = s6 * s * (6.0 - 12.0 * s6)
    t2 = s6 * s_sq * (156.0 * s6 - 42.0)
    ke = (4.0 * well_depth) * e1
    kx = ke * x
    v_ee = kx * (24.0 / cutoff_sq**2)
    kxx = kx * x
    v_e = kxx * (-6.0 / cutoff_sq)
    v = kxx * x
    psi_sq = psi * psi
    psi_sq_t0 = psi_sq * t0
    psi_sq_t1 = psi_sq * t1
    u = v * psi_sq_t0
    slope = v * psi_sq_t1
    slope2 = v * psi_sq * t2
    tau = (-0.5 * chi_shape) * sigma_sq * sigma
    push = (-2.0 * chi_energy) * psi
    v_t1 = v * t1
    d1 = slope * tau
    d2 = push * (v * t0)
    h1 = p2 * d1
    h2 = p2 * d2
    kc = chi_shape * c_shape * q
    fg = chi_shape * f * g
    fg2 = chi_energy * f2 * g2
    u_a = h1 * f + h2 * f2
    u_b = h1 * g + h2 * g2
    u_fg = h1 * fg + h2 * fg2
    u_c = u * kc - u_fg
    v_e_t0 = v_e * psi_sq_t0
    d_e = r_inv * slope + v_e_t0
    u_e = d_e - (h1 * y + h2 * y2)

    p2_sq = p2 * p2
    k11 = p2_sq * (tau * (slope2 * tau + (1.5 * chi_shape) * sigma_sq * slope))
    k12 = p2_sq * (push * v_t1 * tau)
    k22 = p2_sq * ((2.0 * chi_energy * chi_energy) * (v * t0))
    steep = v_e * psi_sq_t1 + slope2 * r_inv
    l1 = p2 * (steep * tau - h1)
    l2 = p2 * (push * (v_e * t0 + v_t1 * r_inv) - h2)
    j1 = (y, f, g, fg)
    j2 = (y2, f2, g2, fg2)
    w1 = [k11 * one + k12 * two for one, two in zip(j1, j2)]
    w2 = [k12 * one + k22 * two for one, two in zip(j1, j2)]

    def quadratic(m_at, n_at):
        return w1[m_at] * j1[n_at] + w2[m_at] * j2[n_at]

    d_ee = v_ee * psi_sq_t0 + r_inv * (2.0 * (v_e * psi_sq_t1)) + p * (slope2 - slope * r_inv)
    h_ee = quadratic(0, 0) - 2.0 * (l1 * y + l2 * y2) + d_ee
    h_ea = l1 * f + l2 * f2 - quadratic(0, 1)
    h_eb = l1 * g + l2 * g2 - quadratic(0, 2)
    h_ec = quadratic(0, 3) - (l1 * fg + l2 * fg2) + kc * u_e
    straight = h1 * q + h2 * q2
    h_aa = quadratic(1, 1) + straight
    h_ab = quadratic(1, 2) - (h1 * m + h2 * m2)
    h_ac = kc * u_a - quadratic(1, 3) + (h1 * f_c + h2 * f2_c)
    h_bb = quadratic(2, 2) + straight
    h_bc = kc * u_b - quadratic(2, 3) + (h1 * g_c + h2 * g2_c)
    bent = (chi_shape * h1) * (f_c * g + f * g_c) + (chi_energy * h2) * (f2_c * g2 + f2 * g2_c)
    twist = kc * kc + (chi_shape * chi_shape) * q * (2.0 * q - 1.0)
    h_cc = quadratic(3, 3) - bent - 2.0 * (kc * u_fg) + u * twist
    gradient = (u_e, u_a, u_b, u_c)
    return gradient, (h_ee, h_ea, h_eb, h_ec, h_aa, h_ab, h_ac, h_bb, h_bc, h_cc), u_a * a + u_c * c


def offsets_of(code, period):
    return [((code >> bits & 3) - 1).astype(jnp.float32) * size for bits, size in zip((4, 2, 0), period)]


def offset_rows(code, period, member):
    row = lax.broadcasted_iota(jnp.int32, (SUB, member), 0)
    shift = offsets_of(code, period)
    third = jnp.where(row == 1, shift[1], shift[2])
    return jnp.where(row < 3, jnp.where(row == 0, shift[0], third), 0.0)


def skew_entry(entry, block, skew_ref):
    for s in range(SUB):
        at = pl.multiple_of(entry * (SUB * SUB) + SUB * s, SUB)
        skew_ref[pl.ds(at, SUB), :] = pltpu.roll(block, s, 1) if s else block


def frame_of(code, period, frame_ref):
    member = frame_ref.shape[2]
    return frame_ref[code >> CODE_BITS] + offset_rows(code, period, member)


def near_blocks(own_frame, partner_frame):
    member = own_frame.shape[1]
    row = lax.broadcasted_iota(jnp.int32, (SUB, member), 0)
    sign = jnp.where(row < 3, 1.0, jnp.where(row < 6, -1.0, 0.0))

    def doubled(block):
        centre = jnp.where(row < 3, block, 0.0)
        return centre + pltpu.roll(centre, 3, 0)

    box = doubled(partner_frame) * sign
    for bit in (1, 2, 4):
        box = jnp.maximum(box, pltpu.roll(box, bit, 1))
    here = doubled(own_frame) * sign
    blocks = member // SUB
    reach = []
    for k in range(blocks):
        gap = jnp.maximum(here - (pltpu.roll(box, k * SUB, 1) if k else box), 0.0)
        reach.append(jnp.sum(gap * gap, axis=0, keepdims=True))
    nearest = jnp.min(jnp.concatenate(reach, axis=0), axis=1, keepdims=True)
    weight = (1 << lax.broadcasted_iota(jnp.int32, (blocks, 1), 0)).astype(jnp.float32)
    return jnp.sum(jnp.where(nearest < cutoff_sq * 1.001, weight, 0.0)).astype(jnp.int32)


def stacked(parts):
    return jnp.concatenate(parts, axis=0)


def wide(block, k):
    return jnp.broadcast_to(block[k : k + 1], (GROUP * SUB, block.shape[1]))


def turned(skew_ref, items, k):
    member = skew_ref.shape[1]
    blocks = member // SUB
    parts = []
    for item in items:
        start = item // blocks * (SUB * SUB) + k
        parts.append(pltpu.roll(skew_ref[pl.ds(start, SUB, stride=SUB), :], item % blocks * SUB, 1))
    return stacked(parts)


def folded(total):
    return jnp.sum(total, axis=0, keepdims=True)


def geometry(items, unused, own_frame, skew_ref):
    member = skew_ref.shape[1]
    first_row = (lax.broadcasted_iota(jnp.int32, (SUB, member), 0) == 0).astype(jnp.float32)
    itself = [jnp.where(item == 0, 2.0 * cutoff_sq, 0.0) for item in items]
    lift = stacked([first_row * one + jnp.where(two, 2.0 * cutoff_sq, 0.0) for one, two in zip(itself, unused)])
    d = [turned(skew_ref, items, k) - wide(own_frame, k) for k in range(3)]
    uj = [turned(skew_ref, items, 3 + k) for k in range(3)]
    ui = [wide(own_frame, 3 + k) for k in range(3)]
    gradient, hessian, spin = pair_coefficients(d, ui, uj, lift)
    return list(gradient) + list(hessian) + d + uj, (gradient[1], spin)


def group_items(step, item_ref, item_count):
    at = [step * GROUP + part for part in range(GROUP)]
    return [item_ref[place] for place in at], [place >= item_count for place in at]


def tile_product(entry_count, item_count, entry_ref, item_ref, coef_ref, kept_ref, own, frame_ref, moved_ref, period, scratch):
    skew_ref, frame_skew_ref = scratch
    member = skew_ref.shape[1]
    own_frame = frame_ref[own]
    own_moved = moved_ref[own]
    held = coef_ref.shape[0] // (TERMS * GROUP * SUB)
    steps = (item_count + GROUP - 1) // GROUP

    def prepare(entry, carry):
        skew_entry(entry, moved_ref[entry_ref[entry] >> CODE_BITS], skew_ref)
        return carry

    lax.fori_loop(0, entry_count, prepare, 0)

    def prepare_frame(entry, carry):
        skew_entry(entry, frame_of(entry_ref[entry], period, frame_ref), frame_skew_ref)
        return carry

    lax.fori_loop(0, jnp.where(steps > held, entry_count, 0), prepare_frame, 0)

    def apply(items, terms, totals):
        u_e, u_a, u_b, u_c, h_ee, h_ea, h_eb, h_ec, h_aa, h_ab, h_ac, h_bb, h_bc, h_cc = terms[:14]
        d = terms[14:17]
        uj = terms[17:20]
        ui = [wide(own_frame, 3 + k) for k in range(3)]
        dui = [wide(own_moved, 3 + k) for k in range(3)]
        dd = [turned(skew_ref, items, k) - wide(own_moved, k) for k in range(3)]
        duj = [turned(skew_ref, items, 3 + k) for k in range(3)]
        de = dot3(d, dd)
        da = dot3(dd, ui) + dot3(d, dui)
        db = dot3(dd, uj) + dot3(d, duj)
        dc = dot3(dui, uj) + dot3(ui, duj)
        du_e = h_ee * de + h_ea * da + h_eb * db + h_ec * dc
        du_a = h_ea * de + h_aa * da + h_ab * db + h_ac * dc
        du_b = h_eb * de + h_ab * da + h_bb * db + h_bc * dc
        du_c = h_ec * de + h_ac * da + h_bc * db + h_cc * dc
        force = [du_e * d[k] + u_e * dd[k] + du_b * uj[k] + u_b * duj[k] for k in range(3)]
        turn = [du_a * d[k] + u_a * dd[k] + du_c * uj[k] + u_c * duj[k] for k in range(3)]
        return tuple(total + new for total, new in zip(totals, force + turn + [du_a]))

    def visit(step, totals):
        items, _ = group_items(step, item_ref, item_count)
        start = pl.multiple_of(step * (TERMS * GROUP * SUB), SUB)
        terms = [coef_ref[pl.ds(start + k * GROUP * SUB, GROUP * SUB), :] for k in range(TERMS)]
        return apply(items, terms, totals)

    def visit_again(step, totals):
        items, unused = group_items(step, item_ref, item_count)
        return apply(items, geometry(items, unused, own_frame, frame_skew_ref)[0], totals)

    zero = jnp.zeros((GROUP * SUB, member), jnp.float32)
    totals = lax.fori_loop(0, jnp.minimum(steps, held), visit, (zero,) * 7)
    totals = lax.fori_loop(held, steps, visit_again, totals)
    sums = [folded(total) for total in totals]
    u = [own_frame[k : k + 1] for k in range(3, 6)]
    t = [own_moved[k : k + 1] for k in range(3, 6)]
    kept = kept_ref[0:1, :]
    spin = kept_ref[1:2, :]
    force = [-(sums[k] + u[k] * sums[6] + t[k] * kept) for k in range(3)]
    turn = cross3(u, [sums[3 + k] - t[k] * spin for k in range(3)])
    return force + list(cross3(turn, u))


def spread(rows, out_ref):
    member = out_ref.shape[2]
    count = sum(row.shape[0] for row in rows)
    fill = [jnp.zeros((1, member), jnp.float32)] * (SUB - count)
    block = jnp.concatenate(list(rows) + fill, axis=0)
    out_ref[...] = jnp.broadcast_to(block[None], out_ref.shape)


def pack_kernel(config_ref, start_ref, list_ref, frame_ref, moved_ref):
    u = [config_ref[k : k + 1, :] for k in range(3, 6)]
    w = [start_ref[k : k + 1, :] for k in range(3, 6)]
    spread([config_ref[...], list_ref[...]], frame_ref)
    spread([start_ref[0:3, :], *cross3(w, u), dot3(w, u)], moved_ref)


def prepare_kernel(
    rows,
    cols,
    slots,
    period,
    frame_ref,
    entry_ref,
    item_ref,
    count_ref,
    coef_ref,
    kept_ref,
    skew_ref,
    code_ref,
    code_smem,
    sem,
):
    member = frame_ref.shape[2]
    row_id = lax.axis_index("row")
    col_id = lax.axis_index("col")
    own = row_id * cols + col_id
    blocks = member // SUB

    def field(line, at):
        return line if at == 0 else pltpu.roll(line, member - at * slots, 1)

    def encode(line, partner, side):
        offset = (field(line, 2) * 16.0 + field(line, 3) * 4.0 + field(line, 4)) * side + 21.0
        return partner * float(1 << CODE_BITS) + offset

    row_f = row_id.astype(jnp.float32)
    col_f = col_id.astype(jnp.float32)
    for col in range(cols):
        line = frame_ref[row_id * cols + col, LIST_ROW : LIST_ROW + 1, :]
        code = encode(line, field(line, 1) * float(cols) + float(col), 1.0)
        code_ref[col : col + 1, :] = jnp.where(line == col_f, code, -1.0).astype(jnp.int32)
    for row in range(rows):
        line = frame_ref[row * cols + col_id, LIST_ROW : LIST_ROW + 1, :]
        code = encode(line, float(row * cols) + line, -1.0)
        hit = (field(line, 1) == row_f) & (line >= 0.0)
        code_ref[cols + row : cols + row + 1, :] = jnp.where(hit, code, -1.0).astype(jnp.int32)
    copy = pltpu.make_async_copy(code_ref, code_smem, sem)
    copy.start()
    copy.wait()

    entry_ref[0] = own * (1 << CODE_BITS) + 21

    def gather(line, count):
        for slot in range(slots):
            code = code_smem[line, slot]
            entry_ref[count] = code
            count = count + (code >= 0).astype(jnp.int32)
        return count

    entries = lax.fori_loop(0, rows + cols, gather, jnp.int32(1))
    own_frame = frame_ref[own]

    def prepare(entry, count):
        frame = frame_of(entry_ref[entry], period, frame_ref)
        skew_entry(entry, frame, skew_ref)
        bits = near_blocks(own_frame, frame)
        for block in range(blocks):
            item_ref[count] = entry * blocks + block
            count = count + (bits >> block & 1)
        return count

    items = lax.fori_loop(0, entries, prepare, jnp.int32(0))
    for part in range(GROUP):
        item_ref[items + part] = 0
    count_ref[0] = entries
    count_ref[1] = items

    held = coef_ref.shape[0] // (TERMS * GROUP * SUB)
    steps = (items + GROUP - 1) // GROUP

    def derive(step, totals):
        group, unused = group_items(step, item_ref, items)
        terms, sums = geometry(group, unused, own_frame, skew_ref)
        return terms, tuple(total + new for total, new in zip(totals, sums))

    def keep(step, totals):
        terms, totals = derive(step, totals)
        start = pl.multiple_of(step * (TERMS * GROUP * SUB), SUB)
        for k in range(TERMS):
            coef_ref[pl.ds(start + k * GROUP * SUB, GROUP * SUB), :] = terms[k]
        return totals

    zero = jnp.zeros((GROUP * SUB, member), jnp.float32)
    totals = lax.fori_loop(0, jnp.minimum(steps, held), keep, (zero,) * 2)
    totals = lax.fori_loop(held, steps, lambda step, before: derive(step, before)[1], totals)
    kept_ref[...] = jnp.concatenate([folded(total) for total in totals], axis=0)


def first_kernel(
    cols,
    period,
    entry_ref,
    item_ref,
    count_ref,
    coef_ref,
    kept_ref,
    frame_ref,
    moved_ref,
    out_ref,
    skew_ref,
    frame_skew_ref,
):
    own = lax.axis_index("row") * cols + lax.axis_index("col")
    product = tile_product(
        count_ref[0],
        count_ref[1],
        entry_ref,
        item_ref,
        coef_ref,
        kept_ref,
        own,
        frame_ref,
        moved_ref,
        period,
        (skew_ref, frame_skew_ref),
    )
    spread(product, out_ref)


def whole_sum(left_ref, right_ref):
    total = jnp.sum(left_ref[...] * right_ref[...], axis=0)
    return jnp.sum(jnp.sum(total, axis=0, keepdims=True), axis=1, keepdims=True)


def scalar_of(block):
    return jnp.sum(jnp.sum(block, axis=0, keepdims=True), axis=1, keepdims=True)


def second_kernel(
    cols,
    total_entries,
    period,
    entry_ref,
    item_ref,
    count_ref,
    coef_ref,
    kept_ref,
    frame_ref,
    basis_ref,
    image_ref,
    out_ref,
    pair_ref,
    scalar_ref,
    second_ref,
    skew_ref,
    frame_skew_ref,
):
    own = lax.axis_index("row") * cols + lax.axis_index("col")
    member = frame_ref.shape[2]
    norm_sq = whole_sum(basis_ref, basis_ref) / total_entries + norm_eps
    alpha = whole_sum(basis_ref, image_ref) / total_entries / norm_sq
    second_ref[...] = image_ref[...] - alpha * basis_ref[...]
    beta = jnp.sqrt(whole_sum(second_ref, second_ref) / total_entries / norm_sq + norm_eps)
    scale = lax.rsqrt(norm_sq) / beta
    product = tile_product(
        count_ref[0],
        count_ref[1],
        entry_ref,
        item_ref,
        coef_ref,
        kept_ref,
        own,
        frame_ref,
        second_ref,
        period,
        (skew_ref, frame_skew_ref),
    )
    fill = [jnp.zeros((1, member), jnp.float32)] * (SUB - len(product))
    image = jnp.concatenate(product + fill, axis=0) * scale - (beta * lax.rsqrt(norm_sq)) * basis_ref[own]
    second = second_ref[own] * scale
    inner = scalar_of(second * image)
    weight = scalar_of(second * second)
    local_alpha = jnp.where(weight > 1e-30, inner / jnp.maximum(weight, 1e-30), 0.0)
    rest = image - local_alpha * second
    size = scalar_of(rest * rest)
    slant = scalar_of(second * rest)
    lane = lax.broadcasted_iota(jnp.int32, (1, member), 1)
    line = jnp.zeros((1, member), jnp.float32)
    for at, value in enumerate((inner, weight, local_alpha, size, slant)):
        line = jnp.where(lane == at, value, line)
    out_ref[...] = jnp.broadcast_to(line[None], out_ref.shape)
    pair_ref[0] = second
    pair_ref[1] = image
    scalar_ref[...] = jnp.where(lane == 0, alpha, jnp.where(lane == 1, beta, 0.0))


def last_kernel(total_entries, config_ref, pair_ref, scalar_ref, line_ref, mode_ref, coefficient_ref):
    lines = line_ref[:, 0, :]
    alpha = jnp.sum(lines[:, 0:1], axis=0, keepdims=True) / total_entries
    away = lines[:, 2:3] - alpha
    parts = lines[:, 3:4] + away * (away * lines[:, 1:2] + 2.0 * lines[:, 4:5])
    beta = jnp.sqrt(jnp.sum(parts, axis=0, keepdims=True) / total_entries + norm_eps)
    mine = (pair_ref[1] - alpha * pair_ref[0]) / beta
    u = [config_ref[k : k + 1, :] for k in range(3, 6)]
    turn = cross3(u, [mine[k : k + 1] for k in range(3, 6)])
    along = mine[6:7]
    mode_ref[...] = jnp.concatenate([mine[0:3]] + [turn[k] + along * u[k] for k in range(3)], axis=0)
    lane = lax.broadcasted_iota(jnp.int32, scalar_ref.shape, 1)
    coefficient_ref[...] = jnp.where(lane == 2, alpha, jnp.where(lane == 3, beta, scalar_ref[...]))


def local(config, start, tile_list, tile_count):
    dof, member = config.shape
    row_devices = lax.axis_size("row")
    col_devices = lax.axis_size("col")
    devices = row_devices * col_devices
    total_entries = float(dof * member * devices)
    period = (5.0, 5.0, 3.5 * (member // 16))
    entries = tile_list[0, 0]
    slots, fields = entries.shape
    longest = (row_devices + col_devices) * slots + 1

    def shaped(*shape):
        return jax.ShapeDtypeStruct(shape, jnp.float32)

    def everywhere(copies):
        return lax.all_to_all(copies, ("row", "col"), 0, 0, tiled=True)

    params = pltpu.CompilerParams(vmem_limit_bytes=VMEM_LIMIT)
    vmem = pl.BlockSpec(memory_space=pltpu.VMEM)
    smem = pl.BlockSpec(memory_space=pltpu.SMEM)

    in_use = jnp.arange(slots, dtype=jnp.int32) < tile_count[0, 0]
    fields_f = jnp.where(in_use[:, None], entries, -9).astype(jnp.float32).T.reshape(1, fields * slots)
    list_row = jnp.pad(fields_f, ((0, 0), (0, member - fields * slots)), constant_values=-9.0)

    frames, basis = pl.pallas_call(
        pack_kernel,
        out_shape=(shaped(devices, SUB, member), shaped(devices, SUB, member)),
        in_specs=[vmem] * 3,
        out_specs=(vmem, vmem),
        compiler_params=params,
    )(config, start, list_row)
    frames = everywhere(frames)
    basis = everywhere(basis)

    skew = pltpu.VMEM((longest * SUB * SUB, member), jnp.float32)
    held_rows = HELD // GROUP * (TERMS * GROUP * SUB)
    codes, items, counts, terms, kept = pl.pallas_call(
        functools.partial(prepare_kernel, row_devices, col_devices, slots, period),
        out_shape=(
            jax.ShapeDtypeStruct((longest + 1,), jnp.int32),
            jax.ShapeDtypeStruct((longest * (member // SUB) + GROUP,), jnp.int32),
            jax.ShapeDtypeStruct((2,), jnp.int32),
            shaped(held_rows, member),
            shaped(2, member),
        ),
        in_specs=[vmem],
        out_specs=(smem, smem, smem, vmem, vmem),
        scratch_shapes=[
            skew,
            pltpu.VMEM((row_devices + col_devices, member), jnp.int32),
            pltpu.SMEM((row_devices + col_devices, member), jnp.int32),
            pltpu.SemaphoreType.DMA,
        ],
        compiler_params=params,
    )(frames)

    image = pl.pallas_call(
        functools.partial(first_kernel, col_devices, period),
        out_shape=shaped(devices, SUB, member),
        in_specs=[smem] * 3 + [vmem] * 4,
        out_specs=vmem,
        scratch_shapes=[skew, skew],
        compiler_params=params,
    )(codes, items, counts, terms, kept, frames, basis)
    image = everywhere(image)

    line, pair, scalars = pl.pallas_call(
        functools.partial(second_kernel, col_devices, total_entries, period),
        out_shape=(shaped(devices, 1, member), shaped(2, SUB, member), shaped(1, member)),
        in_specs=[smem] * 3 + [vmem] * 5,
        out_specs=(vmem, vmem, vmem),
        scratch_shapes=[pltpu.VMEM((devices, SUB, member), jnp.float32), skew, skew],
        compiler_params=params,
    )(codes, items, counts, terms, kept, frames, basis, image)
    line = everywhere(line)

    mode, coefficients = pl.pallas_call(
        functools.partial(last_kernel, total_entries),
        out_shape=(shaped(dof, member), shaped(1, member)),
        in_specs=[vmem] * 4,
        out_specs=(vmem, vmem),
        compiler_params=params,
    )(config, pair, scalars, line)
    return (coefficients[0, :4], mode)


def solution(mesh):
    placed = (
        P(None, ("row", "col")),
        P(None, ("row", "col")),
        P("row", "col", None, None),
        P("row", "col"),
    )
    return jax.shard_map(
        local, mesh=mesh, in_specs=placed, out_specs=(P(), P(None, ("row", "col"))), check_vma=False
    )
```

profile of v0, /device:TPU:0, one launch (start us, length us, event | category | flops | bytes accessed | tf_op | source)
XLA Modules:
  0.0 81.1 jit_solution(16600329729591238082)
XLA Ops:
  1.3 0.8 copy.6
  2.0 0.1 fusion.1
  2.1 0.1 copy.7
  2.2 0.1 reshape.11
  2.3 0.0 copy-start.2
  2.3 0.7 copy-done.2
  3.0 0.0 copy-start.4
  3.0 0.7 copy-done.4
  3.7 0.7 shard_map.59
  4.4 15.3 %all_to_all.20.frame_ref = f32[32,8,128]{2,1,0:T(8,128)S(1)} all-to-all(f32[32,8,128]{2,1,0:T(8,128)S(1)} %get-tuple-element.14), channel_id=1, replica_groups=mesh['row'=4,'col'=8] {'row','col'}, dimensions={0} | all-to-all | bytes 262144 | tf_op jit(solution)/shard_map/all_to_all | solution.py:519
  19.7 2.6 %all-to-all-start.1 = ((f32[32,8,128]{2,1,0:T(8,128)}), f32[32,8,128]{2,1,0:T(8,128)S(1)}, u32[]{:S(2)}, u32[]{:S(2)}) async-start(f32[32,8,128]{2,1,0:T(8,128)} %get-tuple-element.20), calls=%async_computation.1 | async-start | bytes 262144 | tf_op jit(solution)/shard_map/all_to_all | solution.py:519
  22.2 7.7 %shard_map.60 = (s32[98]{0:T(128)S(1)}, s32[1554]{0:T(1024)S(1)}, s32[2]{0:T(128)S(1)}, f32[20480,128]{1,0:T(8,128)S(1)}, f32[2,128]{1,0:T(2,128)S(1)}) custom-call(f32[32,8,128]{2,1,0:T(8,128)S(1)} %all_to_all.20.frame_ref), custom_call_target="tpu_custom_call" | custom-call | tf_op jit(solution)/shard_map/pallas_call | solution.py:541
  29.9 0.0 copy-start
  29.9 4.0 %copy-done = f32[20480,128]{1,0:T(8,128)} copy-done((f32[20480,128]{1,0:T(8,128)}, f32[20480,128]{1,0:T(8,128)S(1)}, u32[]{:S(2)}) %copy-start) | copy-done | bytes 10485784
  33.9 0.0 all-to-all-done.1.moved_ref.basis_ref
  33.9 0.0 copy-start.1
  33.9 4.0 %copy-done.1 = f32[20480,128]{1,0:T(8,128)S(1)} copy-done((f32[20480,128]{1,0:T(8,128)S(1)}, f32[20480,128]{1,0:T(8,128)}, u32[]{:S(2)}) %copy-start.1) | copy-done | bytes 10485784
  37.9 0.0 copy-start.3
  37.9 3.6 %shard_map.61 = f32[32,8,128]{2,1,0:T(8,128)S(1)} custom-call(s32[98]{0:T(128)S(1)} %get-tuple-element.15.entry_ref, s32[1554]{0:T(1024)S(1)} %get-tuple-element.16.item_ref, s32[2]{0:T(128)S(1)} %get-tuple-element.17.count_ref, f32[20480,128]{1,0:T(8,128)S(1)} %copy-done.1, f32[2,128]{1,0:T(2,128)S(1)} %get-tuple-element.19.kept_ref, ...), custom_call_target="tpu_custom_call" | custom-call | tf_op jit(solution)/shard_map/pallas_call | solution.py:561
  41.5 22.8 %all_to_all.21.image_ref = f32[32,8,128]{2,1,0:T(8,128)S(1)} all-to-all(f32[32,8,128]{2,1,0:T(8,128)S(1)} %shard_map.61), channel_id=1, replica_groups=mesh['row'=4,'col'=8] {'row','col'}, dimensions={0} | all-to-all | bytes 262144 | tf_op jit(solution)/shard_map/all_to_all | solution.py:519
  64.4 4.0 %shard_map.62 = (f32[32,1,128]{2,1,0:T(1,128)S(1)}, f32[2,8,128]{2,1,0:T(8,128)S(1)}, f32[1,128]{1,0:T(1,128)S(1)}) custom-call(s32[98]{0:T(128)S(1)} %get-tuple-element.15.entry_ref, s32[1554]{0:T(1024)S(1)} %get-tuple-element.16.item_ref, s32[2]{0:T(128)S(1)} %get-tuple-element.17.count_ref, f32[20480,128]{1,0:T(8,128)S(1)} %copy-done.1, ...), custom_call_target="tpu_custom_call" | custom-call | tf_op jit(solution)/shard_map/pallas_call | solution.py:571
  68.4 11.4 %all_to_all.22.line_ref = f32[32,1,128]{2,1,0:T(1,128)S(1)} all-to-all(f32[32,1,128]{2,1,0:T(1,128)S(1)} %get-tuple-element.23), channel_id=1, replica_groups=mesh['row'=4,'col'=8] {'row','col'}, dimensions={0} | all-to-all | bytes 32768 | tf_op jit(solution)/shard_map/all_to_all | solution.py:519
  79.8 0.0 copy-done.3
  79.8 0.8 shard_map.63
  80.6 0.5 slice_bitcast_fusion
  (2 shorter events, 0.0 us)
Async XLA Ops:
  2.3 0.7 copy-start.2
  3.0 0.7 copy-start.4
  19.7 14.2 %all-to-all-start.1 = ((f32[32,8,128]{2,1,0:T(8,128)}), f32[32,8,128]{2,1,0:T(8,128)S(1)}, u32[]{:S(2)}, u32[]{:S(2)}) async-start(f32[32,8,128]{2,1,0:T(8,128)} %get-tuple-element.20), calls=%async_computation.1 | async-start | bytes 262144 | tf_op jit(solution)/shard_map/all_to_all | solution.py:519
  29.9 4.0 %copy-start = (f32[20480,128]{1,0:T(8,128)}, f32[20480,128]{1,0:T(8,128)S(1)}, u32[]{:S(2)}) copy-start(f32[20480,128]{1,0:T(8,128)S(1)} %get-tuple-element.18.coef_ref) | copy-start | bytes 31457284
  33.9 4.0 %copy-start.1 = (f32[20480,128]{1,0:T(8,128)S(1)}, f32[20480,128]{1,0:T(8,128)}, u32[]{:S(2)}) copy-start(f32[20480,128]{1,0:T(8,128)} %copy-done) | copy-start | bytes 31457284
  37.9 41.9 %copy-start.3 = (f32[6,128]{1,0:T(8,128)S(1)}, f32[6,128]{1,0:T(8,128)}, u32[]{:S(2)}) copy-start(f32[6,128]{1,0:T(8,128)} %config_ref.3) | copy-start | bytes 9220
where the time goes:
time: 80.3 us; the launch traced here: 81.1 us
  blocking collectives  49.5 us (62%)
  Pallas kernels  16.8 us (21%)
  local copies, waits for them, and re-layouts  10.8 us (13%)
  starting transfers between devices  2.55 us (3%)
  between operations  1.33 us (2%)
    all_to_all x3, blocking collectives, everywhere(): return lax.all_to_all(copies, ('row', 'col'), 0, 0, tiled=True)  49.5 us
    unnamed x11, local copies, waits for them, and re-layouts  10.1 us
    pallas_call x1, Pallas kernels, local(): pl.pallas_call(functools.partial(prepare_kernel, row_devices, col_devices...  7.67 us
    pallas_call x1, Pallas kernels, local(): pl.pallas_call(functools.partial(second_kernel, col_devices, total_entrie...  4.04 us
    pallas_call x1, Pallas kernels, local(): pl.pallas_call(functools.partial(first_kernel, col_devices, period), out_...  3.63 us
    all_to_all x1, starting transfers between devices, everywhere(): return lax.all_to_all(copies, ('row', 'col'), 0, 0, tiled=True)  2.55 us
  transfers between devices with their start and end apart: 1, of which 0 were waited for; matrix products, arithmetic and copies ran while one was open for 0% of the time, Pallas kernels for 9%

commit v1 on v0

--- a/solution.py
+++ b/solution.py
@@ -15,8 +15,10 @@
 norm_eps = 1e-06
 
 SUB = 8
-LIST_ROW = 6
+LIST_ROW = 14
 CODE_BITS = 6
+ITEM_BITS = 8
+ITEM_MASK = 255
 GROUP = 2
 TERMS = 20
 HELD = 128
@@ -147,13 +149,12 @@
 
 def skew_entry(entry, block, skew_ref):
     for s in range(SUB):
-        at = pl.multiple_of(entry * (SUB * SUB) + SUB * s, SUB)
-        skew_ref[pl.ds(at, SUB), :] = pltpu.roll(block, s, 1) if s else block
-
-
-def frame_of(code, period, frame_ref):
-    member = frame_ref.shape[2]
-    return frame_ref[code >> CODE_BITS] + offset_rows(code, period, member)
+        at = entry * (SUB * SUB) + s
+        skew_ref[pl.ds(at, SUB, stride=SUB), :] = pltpu.roll(block, s, 1) if s else block
+
+
+def frame_of(code, period, all_ref):
+    return all_ref[code >> CODE_BITS, SUB : 2 * SUB, :] + offset_rows(code, period, all_ref.shape[2])
 
 
 def near_blocks(own_frame, partner_frame):
@@ -188,12 +189,10 @@
 
 
 def turned(skew_ref, items, k):
-    member = skew_ref.shape[1]
-    blocks = member // SUB
     parts = []
     for item in items:
-        start = item // blocks * (SUB * SUB) + k
-        parts.append(pltpu.roll(skew_ref[pl.ds(start, SUB, stride=SUB), :], item % blocks * SUB, 1))
+        start = pl.multiple_of((item >> ITEM_BITS) * (SUB * SUB) + k * SUB, SUB)
+        parts.append(pltpu.roll(skew_ref[pl.ds(start, SUB), :], item & ITEM_MASK, 1))
     return stacked(parts)
 
 
@@ -201,16 +200,36 @@
     return jnp.sum(total, axis=0, keepdims=True)
 
 
-def geometry(items, unused, own_frame, skew_ref):
+def geometry(items, unused, own_wide, skew_ref):
     member = skew_ref.shape[1]
     first_row = (lax.broadcasted_iota(jnp.int32, (SUB, member), 0) == 0).astype(jnp.float32)
     itself = [jnp.where(item == 0, 2.0 * cutoff_sq, 0.0) for item in items]
     lift = stacked([first_row * one + jnp.where(two, 2.0 * cutoff_sq, 0.0) for one, two in zip(itself, unused)])
-    d = [turned(skew_ref, items, k) - wide(own_frame, k) for k in range(3)]
+    d = [turned(skew_ref, items, k) - own_wide[k] for k in range(3)]
     uj = [turned(skew_ref, items, 3 + k) for k in range(3)]
-    ui = [wide(own_frame, 3 + k) for k in range(3)]
-    gradient, hessian, spin = pair_coefficients(d, ui, uj, lift)
+    gradient, hessian, spin = pair_coefficients(d, own_wide[3:], uj, lift)
     return list(gradient) + list(hessian) + d + uj, (gradient[1], spin)
+
+
+def apply(items, terms, own_wide, moved_wide, skew_ref):
+    u_e, u_a, u_b, u_c, h_ee, h_ea, h_eb, h_ec, h_aa, h_ab, h_ac, h_bb, h_bc, h_cc = terms[:14]
+    d = terms[14:17]
+    uj = terms[17:20]
+    ui = own_wide[3:]
+    dui = moved_wide[3:]
+    dd = [turned(skew_ref, items, k) - moved_wide[k] for k in range(3)]
+    duj = [turned(skew_ref, items, 3 + k) for k in range(3)]
+    de = dot3(d, dd)
+    da = dot3(dd, ui) + dot3(d, dui)
+    db = dot3(dd, uj) + dot3(d, duj)
+    dc = dot3(dui, uj) + dot3(ui, duj)
+    du_e = h_ee * de + h_ea * da + h_eb * db + h_ec * dc
+    du_a = h_ea * de + h_aa * da + h_ab * db + h_ac * dc
+    du_b = h_eb * de + h_ab * da + h_bb * db + h_bc * dc
+    du_c = h_ec * de + h_ac * da + h_bc * db + h_cc * dc
+    force = [du_e * d[k] + u_e * dd[k] + du_b * uj[k] + u_b * duj[k] for k in range(3)]
+    turn = [du_a * d[k] + u_a * dd[k] + du_c * uj[k] + u_c * duj[k] for k in range(3)]
+    return force + turn + [du_a]
 
 
 def group_items(step, item_ref, item_count):
@@ -218,64 +237,15 @@
     return [item_ref[place] for place in at], [place >= item_count for place in at]
 
 
-def tile_product(entry_count, item_count, entry_ref, item_ref, coef_ref, kept_ref, own, frame_ref, moved_ref, period, scratch):
-    skew_ref, frame_skew_ref = scratch
-    member = skew_ref.shape[1]
-    own_frame = frame_ref[own]
-    own_moved = moved_ref[own]
-    held = coef_ref.shape[0] // (TERMS * GROUP * SUB)
-    steps = (item_count + GROUP - 1) // GROUP
-
-    def prepare(entry, carry):
-        skew_entry(entry, moved_ref[entry_ref[entry] >> CODE_BITS], skew_ref)
-        return carry
-
-    lax.fori_loop(0, entry_count, prepare, 0)
-
-    def prepare_frame(entry, carry):
-        skew_entry(entry, frame_of(entry_ref[entry], period, frame_ref), frame_skew_ref)
-        return carry
-
-    lax.fori_loop(0, jnp.where(steps > held, entry_count, 0), prepare_frame, 0)
-
-    def apply(items, terms, totals):
-        u_e, u_a, u_b, u_c, h_ee, h_ea, h_eb, h_ec, h_aa, h_ab, h_ac, h_bb, h_bc, h_cc = terms[:14]
-        d = terms[14:17]
-        uj = terms[17:20]
-        ui = [wide(own_frame, 3 + k) for k in range(3)]
-        dui = [wide(own_moved, 3 + k) for k in range(3)]
-        dd = [turned(skew_ref, items, k) - wide(own_moved, k) for k in range(3)]
-        duj = [turned(skew_ref, items, 3 + k) for k in range(3)]
-        de = dot3(d, dd)
-        da = dot3(dd, ui) + dot3(d, dui)
-        db = dot3(dd, uj) + dot3(d, duj)
-        dc = dot3(dui, uj) + dot3(ui, duj)
-        du_e = h_ee * de + h_ea * da + h_eb * db + h_ec * dc
-        du_a = h_ea * de + h_aa * da + h_ab * db + h_ac * dc
-        du_b = h_eb * de + h_ab * da + h_bb * db + h_bc * dc
-        du_c = h_ec * de + h_ac * da + h_bc * db + h_cc * dc
-        force = [du_e * d[k] + u_e * dd[k] + du_b * uj[k] + u_b * duj[k] for k in range(3)]
-        turn = [du_a * d[k] + u_a * dd[k] + du_c * uj[k] + u_c * duj[k] for k in range(3)]
-        return tuple(total + new for total, new in zip(totals, force + turn + [du_a]))
-
-    def visit(step, totals):
-        items, _ = group_items(step, item_ref, item_count)
-        start = pl.multiple_of(step * (TERMS * GROUP * SUB), SUB)
-        terms = [coef_ref[pl.ds(start + k * GROUP * SUB, GROUP * SUB), :] for k in range(TERMS)]
-        return apply(items, terms, totals)
-
-    def visit_again(step, totals):
-        items, unused = group_items(step, item_ref, item_count)
-        return apply(items, geometry(items, unused, own_frame, frame_skew_ref)[0], totals)
-
-    zero = jnp.zeros((GROUP * SUB, member), jnp.float32)
-    totals = lax.fori_loop(0, jnp.minimum(steps, held), visit, (zero,) * 7)
-    totals = lax.fori_loop(held, steps, visit_again, totals)
-    sums = [folded(total) for total in totals]
+def added(totals, news):
+    return tuple(
+        total + sum(new[part * SUB : (part + 1) * SUB] for part in range(GROUP)) for total, new in zip(totals, news)
+    )
+
+
+def close(sums, kept, spin, own_frame, own_moved):
     u = [own_frame[k : k + 1] for k in range(3, 6)]
     t = [own_moved[k : k + 1] for k in range(3, 6)]
-    kept = kept_ref[0:1, :]
-    spin = kept_ref[1:2, :]
     force = [-(sums[k] + u[k] * sums[6] + t[k] * kept) for k in range(3)]
     turn = cross3(u, [sums[3 + k] - t[k] * spin for k in range(3)])
     return force + list(cross3(turn, u))
@@ -284,35 +254,38 @@
 def spread(rows, out_ref):
     member = out_ref.shape[2]
     count = sum(row.shape[0] for row in rows)
-    fill = [jnp.zeros((1, member), jnp.float32)] * (SUB - count)
+    fill = [jnp.zeros((1, member), jnp.float32)] * (out_ref.shape[1] - count)
     block = jnp.concatenate(list(rows) + fill, axis=0)
     out_ref[...] = jnp.broadcast_to(block[None], out_ref.shape)
 
 
-def pack_kernel(config_ref, start_ref, list_ref, frame_ref, moved_ref):
+def pack_kernel(config_ref, start_ref, list_ref, out_ref):
+    member = out_ref.shape[2]
     u = [config_ref[k : k + 1, :] for k in range(3, 6)]
     w = [start_ref[k : k + 1, :] for k in range(3, 6)]
-    spread([config_ref[...], list_ref[...]], frame_ref)
-    spread([start_ref[0:3, :], *cross3(w, u), dot3(w, u)], moved_ref)
-
-
-def prepare_kernel(
+    zero = jnp.zeros((1, member), jnp.float32)
+    spread([start_ref[0:3, :], *cross3(w, u), dot3(w, u), zero, config_ref[...], list_ref[...], zero], out_ref)
+
+
+def first_kernel(
     rows,
     cols,
     slots,
     period,
-    frame_ref,
+    all_ref,
+    out_ref,
     entry_ref,
     item_ref,
     count_ref,
     coef_ref,
     kept_ref,
     skew_ref,
+    frame_skew_ref,
     code_ref,
     code_smem,
     sem,
 ):
-    member = frame_ref.shape[2]
+    member = all_ref.shape[2]
     row_id = lax.axis_index("row")
     col_id = lax.axis_index("col")
     own = row_id * cols + col_id
@@ -328,11 +301,11 @@
     row_f = row_id.astype(jnp.float32)
     col_f = col_id.astype(jnp.float32)
     for col in range(cols):
-        line = frame_ref[row_id * cols + col, LIST_ROW : LIST_ROW + 1, :]
+        line = all_ref[row_id * cols + col, LIST_ROW : LIST_ROW + 1, :]
         code = encode(line, field(line, 1) * float(cols) + float(col), 1.0)
         code_ref[col : col + 1, :] = jnp.where(line == col_f, code, -1.0).astype(jnp.int32)
     for row in range(rows):
-        line = frame_ref[row * cols + col_id, LIST_ROW : LIST_ROW + 1, :]
+        line = all_ref[row * cols + col_id, LIST_ROW : LIST_ROW + 1, :]
         code = encode(line, float(row * cols) + line, -1.0)
         hit = (field(line, 1) == row_f) & (line >= 0.0)
         code_ref[cols + row : cols + row + 1, :] = jnp.where(hit, code, -1.0).astype(jnp.int32)
@@ -350,14 +323,17 @@
         return count
 
     entries = lax.fori_loop(0, rows + cols, gather, jnp.int32(1))
-    own_frame = frame_ref[own]
+    own_frame = all_ref[own, SUB : 2 * SUB, :]
+    own_moved = all_ref[own, 0:SUB, :]
 
     def prepare(entry, count):
-        frame = frame_of(entry_ref[entry], period, frame_ref)
-        skew_entry(entry, frame, skew_ref)
+        code = entry_ref[entry]
+        frame = frame_of(code, period, all_ref)
+        skew_entry(entry, frame, frame_skew_ref)
+        skew_entry(entry, all_ref[code >> CODE_BITS, 0:SUB, :], skew_ref)
         bits = near_blocks(own_frame, frame)
         for block in range(blocks):
-            item_ref[count] = entry * blocks + block
+            item_ref[count] = (entry << ITEM_BITS) + block * SUB
             count = count + (bits >> block & 1)
         return count
 
@@ -369,11 +345,13 @@
 
     held = coef_ref.shape[0] // (TERMS * GROUP * SUB)
     steps = (items + GROUP - 1) // GROUP
+    own_wide = [wide(own_frame, k) for k in range(6)]
+    moved_wide = [wide(own_moved, k) for k in range(6)]
 
     def derive(step, totals):
         group, unused = group_items(step, item_ref, items)
-        terms, sums = geometry(group, unused, own_frame, skew_ref)
-        return terms, tuple(total + new for total, new in zip(totals, sums))
+        terms, sums = geometry(group, unused, own_wide, frame_skew_ref)
+        return terms, added(totals, apply(group, terms, own_wide, moved_wide, skew_ref) + list(sums))
 
     def keep(step, totals):
         terms, totals = derive(step, totals)
@@ -382,41 +360,12 @@
             coef_ref[pl.ds(start + k * GROUP * SUB, GROUP * SUB), :] = terms[k]
         return totals
 
-    zero = jnp.zeros((GROUP * SUB, member), jnp.float32)
-    totals = lax.fori_loop(0, jnp.minimum(steps, held), keep, (zero,) * 2)
+    zero = jnp.zeros((SUB, member), jnp.float32)
+    totals = lax.fori_loop(0, jnp.minimum(steps, held), keep, (zero,) * 9)
     totals = lax.fori_loop(held, steps, lambda step, before: derive(step, before)[1], totals)
-    kept_ref[...] = jnp.concatenate([folded(total) for total in totals], axis=0)
-
-
-def first_kernel(
-    cols,
-    period,
-    entry_ref,
-    item_ref,
-    count_ref,
-    coef_ref,
-    kept_ref,
-    frame_ref,
-    moved_ref,
-    out_ref,
-    skew_ref,
-    frame_skew_ref,
-):
-    own = lax.axis_index("row") * cols + lax.axis_index("col")
-    product = tile_product(
-        count_ref[0],
-        count_ref[1],
-        entry_ref,
-        item_ref,
-        coef_ref,
-        kept_ref,
-        own,
-        frame_ref,
-        moved_ref,
-        period,
-        (skew_ref, frame_skew_ref),
-    )
-    spread(product, out_ref)
+    sums = [folded(total) for total in totals]
+    kept_ref[...] = jnp.concatenate(sums[7:], axis=0)
+    spread(close(sums, sums[7], sums[8], own_frame, own_moved), out_ref)
 
 
 def whole_sum(left_ref, right_ref):
@@ -437,36 +386,63 @@
     count_ref,
     coef_ref,
     kept_ref,
-    frame_ref,
-    basis_ref,
+    all_ref,
     image_ref,
     out_ref,
     pair_ref,
     scalar_ref,
+    basis_ref,
     second_ref,
     skew_ref,
     frame_skew_ref,
 ):
     own = lax.axis_index("row") * cols + lax.axis_index("col")
-    member = frame_ref.shape[2]
+    member = all_ref.shape[2]
+    basis_ref[...] = all_ref[:, 0:SUB, :]
     norm_sq = whole_sum(basis_ref, basis_ref) / total_entries + norm_eps
     alpha = whole_sum(basis_ref, image_ref) / total_entries / norm_sq
     second_ref[...] = image_ref[...] - alpha * basis_ref[...]
     beta = jnp.sqrt(whole_sum(second_ref, second_ref) / total_entries / norm_sq + norm_eps)
     scale = lax.rsqrt(norm_sq) / beta
-    product = tile_product(
-        count_ref[0],
-        count_ref[1],
-        entry_ref,
-        item_ref,
-        coef_ref,
-        kept_ref,
-        own,
-        frame_ref,
-        second_ref,
-        period,
-        (skew_ref, frame_skew_ref),
-    )
+
+    entries = count_ref[0]
+    items = count_ref[1]
+    held = coef_ref.shape[0] // (TERMS * GROUP * SUB)
+    steps = (items + GROUP - 1) // GROUP
+
+    def prepare(entry, carry):
+        skew_entry(entry, second_ref[entry_ref[entry] >> CODE_BITS], skew_ref)
+        return carry
+
+    lax.fori_loop(0, entries, prepare, 0)
+
+    def prepare_frame(entry, carry):
+        skew_entry(entry, frame_of(entry_ref[entry], period, all_ref), frame_skew_ref)
+        return carry
+
+    lax.fori_loop(0, jnp.where(steps > held, entries, 0), prepare_frame, 0)
+
+    own_frame = all_ref[own, SUB : 2 * SUB, :]
+    own_moved = second_ref[own]
+    own_wide = [wide(own_frame, k) for k in range(6)]
+    moved_wide = [wide(own_moved, k) for k in range(6)]
+
+    def visit(step, totals):
+        group, _ = group_items(step, item_ref, items)
+        start = pl.multiple_of(step * (TERMS * GROUP * SUB), SUB)
+        terms = [coef_ref[pl.ds(start + k * GROUP * SUB, GROUP * SUB), :] for k in range(TERMS)]
+        return added(totals, apply(group, terms, own_wide, moved_wide, skew_ref))
+
+    def visit_again(step, totals):
+        group, unused = group_items(step, item_ref, items)
+        terms, _ = geometry(group, unused, own_wide, frame_skew_ref)
+        return added(totals, apply(group, terms, own_wide, moved_wide, skew_ref))
+
+    zero = jnp.zeros((SUB, member), jnp.float32)
+    totals = lax.fori_loop(0, jnp.minimum(steps, held), visit, (zero,) * 7)
+    totals = lax.fori_loop(held, steps, visit_again, totals)
+    sums = [folded(total) for total in totals]
+    product = close(sums, kept_ref[0:1, :], kept_ref[1:2, :], own_frame, own_moved)
     fill = [jnp.zeros((1, member), jnp.float32)] * (SUB - len(product))
     image = jnp.concatenate(product + fill, axis=0) * scale - (beta * lax.rsqrt(norm_sq)) * basis_ref[own]
     second = second_ref[own] * scale
@@ -526,21 +502,21 @@
     fields_f = jnp.where(in_use[:, None], entries, -9).astype(jnp.float32).T.reshape(1, fields * slots)
     list_row = jnp.pad(fields_f, ((0, 0), (0, member - fields * slots)), constant_values=-9.0)
 
-    frames, basis = pl.pallas_call(
+    packed = pl.pallas_call(
         pack_kernel,
-        out_shape=(shaped(devices, SUB, member), shaped(devices, SUB, member)),
+        out_shape=shaped(devices, 2 * SUB, member),
         in_specs=[vmem] * 3,
-        out_specs=(vmem, vmem),
+        out_specs=vmem,
         compiler_params=params,
     )(config, start, list_row)
-    frames = everywhere(frames)
-    basis = everywhere(basis)
+    together = everywhere(packed)
 
     skew = pltpu.VMEM((longest * SUB * SUB, member), jnp.float32)
     held_rows = HELD // GROUP * (TERMS * GROUP * SUB)
-    codes, items, counts, terms, kept = pl.pallas_call(
-        functools.partial(prepare_kernel, row_devices, col_devices, slots, period),
+    image, codes, items, counts, terms, kept = pl.pallas_call(
+        functools.partial(first_kernel, row_devices, col_devices, slots, period),
         out_shape=(
+            shaped(devices, SUB, member),
             jax.ShapeDtypeStruct((longest + 1,), jnp.int32),
             jax.ShapeDtypeStruct((longest * (member // SUB) + GROUP,), jnp.int32),
             jax.ShapeDtypeStruct((2,), jnp.int32),
@@ -548,34 +524,31 @@
             shaped(2, member),
         ),
         in_specs=[vmem],
-        out_specs=(smem, smem, smem, vmem, vmem),
+        out_specs=(vmem, smem, smem, smem, vmem, vmem),
         scratch_shapes=[
+            skew,
             skew,
             pltpu.VMEM((row_devices + col_devices, member), jnp.int32),
             pltpu.SMEM((row_devices + col_devices, member), jnp.int32),
             pltpu.SemaphoreType.DMA,
         ],
         compiler_params=params,
-    )(frames)
-
-    image = pl.pallas_call(
-        functools.partial(first_kernel, col_devices, period),
-        out_shape=shaped(devices, SUB, member),
-        in_specs=[smem] * 3 + [vmem] * 4,
-        out_specs=vmem,
-        scratch_shapes=[skew, skew],
-        compiler_params=params,
-    )(codes, items, counts, terms, kept, frames, basis)
+    )(together)
     image = everywhere(image)
 
     line, pair, scalars = pl.pallas_call(
         functools.partial(second_kernel, col_devices, total_entries, period),
         out_shape=(shaped(devices, 1, member), shaped(2, SUB, member), shaped(1, member)),
-        in_specs=[smem] * 3 + [vmem] * 5,
+        in_specs=[smem] * 3 + [vmem] * 4,
         out_specs=(vmem, vmem, vmem),
-        scratch_shapes=[pltpu.VMEM((devices, SUB, member), jnp.float32), skew, skew],
+        scratch_shapes=[
+            pltpu.VMEM((devices, SUB, member), jnp.float32),
+            pltpu.VMEM((devices, SUB, member), jnp.float32),
+            skew,
+            skew,
+        ],
         compiler_params=params,
-    )(codes, items, counts, terms, kept, frames, basis, image)
+    )(codes, items, counts, terms, kept, together, image)
     line = everywhere(line)
 
     mode, coefficients = pl.pallas_call(

time: 80.3 us -> 62.9 us (0.78); the launches traced: 81.1 us -> 62.8 us
  local copies, waits for them, and re-layouts: 10.8 us -> 2.82 us
  Pallas kernels: 16.8 us -> 11 us
  starting transfers between devices: 2.55 us -> 0 us
  blocking collectives: 49.5 us -> 47.6 us
    unnamed x11 -> x7, local copies, waits for them, and re-layouts: 10.1 us -> 2.14 us
    pallas_call x3 -> x2, Pallas kernels: 12 us -> 7.19 us  [the longest x1 7.17 us: local(): pl.pallas_call(functools.partial(first_kernel, row_devices, col_devices,...]
    all_to_all x1 -> x0, starting transfers between devices: 2.55 us -> none  [everywhere(): return lax.all_to_all(copies, ('row', 'col'), 0, 0, tiled=True)]
    all_to_all x3, blocking collectives: 49.5 us -> 47.6 us  [everywhere(): return lax.all_to_all(copies, ('row', 'col'), 0, 0, tiled=True)]
    pallas_call x1, Pallas kernels: 4.04 us -> 2.98 us  [local(): pl.pallas_call(functools.partial(second_kernel, col_devices, total_entrie...]
  transfers between devices with their start and end apart: 1 -> 0, of which waited for: 0 -> 0; matrix products, arithmetic and copies ran while one was open for 0% -> 0% of each run, Pallas kernels for 9% -> 0%
where the time goes in v1:
time: 62.9 us; the launch traced here: 62.8 us
  blocking collectives  47.6 us (76%)
  Pallas kernels  11 us (17%)
  local copies, waits for them, and re-layouts  2.82 us (4%)
  between operations  1.33 us (2%)
    all_to_all x3, blocking collectives, everywhere(): return lax.all_to_all(copies, ('row', 'col'), 0, 0, tiled=True)  47.6 us
    pallas_call x1, Pallas kernels, local(): pl.pallas_call(functools.partial(first_kernel, row_devices, col_devices,...  7.17 us
    pallas_call x1, Pallas kernels, local(): pl.pallas_call(functools.partial(second_kernel, col_devices, total_entrie...  2.98 us
    unnamed x7, local copies, waits for them, and re-layouts  2.14 us

profile of v1, /device:TPU:0, one launch (start us, length us, event | category | flops | bytes accessed | tf_op | source)
XLA Modules:
  0.0 62.8 jit_solution(8056741971736726528)
XLA Ops:
  0.6 0.0 copy-start.1
  1.3 0.8 %copy.6 = s32[1,1,8,5]{3,2,1,0:T(8,128)S(1)} copy(s32[1,1,8,5]{2,1,3,0:T(1,128)} %param.6) | data formatting | bytes 320 | tf_op args[2]
  2.1 0.1 fusion.1
  2.1 0.1 copy.7
  2.2 0.1 reshape.11
  2.3 0.0 copy-start
  2.3 0.7 %copy-done = f32[6,128]{1,0:T(8,128)S(1)} copy-done((f32[6,128]{1,0:T(8,128)S(1)}, f32[6,128]{1,0:T(8,128)}, u32[]{:S(2)}) %copy-start) | copy-done | bytes 3096
  3.0 0.0 copy-start.2
  3.0 0.7 %copy-done.2 = f32[6,128]{1,0:T(8,128)S(1)} copy-done((f32[6,128]{1,0:T(8,128)S(1)}, f32[6,128]{1,0:T(8,128)}, u32[]{:S(2)}) %copy-start.2) | copy-done | bytes 3096
  3.7 17.7 %all_to_all.15.all_ref = f32[32,16,128]{2,1,0:T(8,128)S(1)} all-to-all(f32[32,16,128]{2,1,0:T(8,128)S(1)} %shard_map.59), channel_id=1, replica_groups=mesh['row'=4,'col'=8] {'row','col'}, dimensions={0} | all-to-all | bytes 524288 | tf_op jit(solution)/shard_map/all_to_all | solution.py:495
  21.4 7.2 %shard_map.60 = (f32[32,8,128]{2,1,0:T(8,128)S(1)}, s32[98]{0:T(128)S(1)}, s32[1554]{0:T(1024)S(1)}, s32[2]{0:T(128)S(1)}, f32[20480,128]{1,0:T(8,128)S(1)}, /*index=5*/f32[2,128]{1,0:T(2,128)S(1)}) custom-call(f32[32,16,128]{2,1,0:T(8,128)S(1)} %all_to_all.15.all_ref), custom_call_target="tpu_custom_call" | custom-call | tf_op jit(solution)/shard_map/pallas_call | solution.py:516
  28.6 17.7 %all_to_all.16.image_ref = f32[32,8,128]{2,1,0:T(8,128)S(1)} all-to-all(f32[32,8,128]{2,1,0:T(8,128)S(1)} %get-tuple-element.18), channel_id=1, replica_groups=mesh['row'=4,'col'=8] {'row','col'}, dimensions={0} | all-to-all | bytes 262144 | tf_op jit(solution)/shard_map/all_to_all | solution.py:495
  46.3 3.0 %shard_map.61 = (f32[32,1,128]{2,1,0:T(1,128)S(1)}, f32[2,8,128]{2,1,0:T(8,128)S(1)}, f32[1,128]{1,0:T(1,128)S(1)}) custom-call(s32[98]{0:T(128)S(1)} %get-tuple-element.13.entry_ref, s32[1554]{0:T(1024)S(1)} %get-tuple-element.14.item_ref, s32[2]{0:T(128)S(1)} %get-tuple-element.15.count_ref, f32[20480,128]{1,0:T(8,128)S(1)} %get-tuple-element.16.coef_ref, ...), custom_call_target="tpu_custom_call" | custom-call | tf_op jit(solution)/shard_map/pallas_call | solution.py:539
  49.3 12.2 %all_to_all.17.line_ref = f32[32,1,128]{2,1,0:T(1,128)S(1)} all-to-all(f32[32,1,128]{2,1,0:T(1,128)S(1)} %get-tuple-element.21), channel_id=1, replica_groups=mesh['row'=4,'col'=8] {'row','col'}, dimensions={0} | all-to-all | bytes 32768 | tf_op jit(solution)/shard_map/all_to_all | solution.py:495
  61.5 0.0 copy-done.1
  61.5 0.8 %shard_map.62 = (f32[6,128]{1,0:T(8,128)}, f32[1,128]{1,0:T(1,128)S(1)}) custom-call(f32[6,128]{1,0:T(8,128)S(1)} %copy-done.1, f32[2,8,128]{2,1,0:T(8,128)S(1)} %get-tuple-element.19.pair_ref, f32[1,128]{1,0:T(1,128)S(1)} %get-tuple-element.20.scalar_ref, f32[32,1,128]{2,1,0:T(1,128)S(1)} %all_to_all.17.line_ref), custom_call_target="tpu_custom_call" | custom-call | tf_op jit(solution)/shard_map/pallas_call | solution.py:554
  62.3 0.5 slice_bitcast_fusion
  (3 shorter events, 0.0 us)
Async XLA Ops:
  0.6 60.9 %copy-start.1 = (f32[6,128]{1,0:T(8,128)S(1)}, f32[6,128]{1,0:T(8,128)}, u32[]{:S(2)}) copy-start(f32[6,128]{1,0:T(8,128)} %config_ref.3) | copy-start | bytes 9220
  2.3 0.7 %copy-start = (f32[6,128]{1,0:T(8,128)S(1)}, f32[6,128]{1,0:T(8,128)}, u32[]{:S(2)}) copy-start(f32[6,128]{1,0:T(8,128)} %config_ref.3) | copy-start | bytes 9220
  3.0 0.7 %copy-start.2 = (f32[6,128]{1,0:T(8,128)S(1)}, f32[6,128]{1,0:T(8,128)}, u32[]{:S(2)}) copy-start(f32[6,128]{1,0:T(8,128)} %start_ref.1) | copy-start | bytes 9220

commit v2 on v1

--- a/solution.py
+++ b/solution.py
@@ -19,6 +19,7 @@
 CODE_BITS = 6
 ITEM_BITS = 8
 ITEM_MASK = 255
+LAYER = 16
 GROUP = 2
 TERMS = 20
 HELD = 128
@@ -147,17 +148,22 @@
     return jnp.where(row < 3, jnp.where(row == 0, shift[0], third), 0.0)
 
 
-def skew_entry(entry, block, skew_ref):
-    for s in range(SUB):
-        at = entry * (SUB * SUB) + s
-        skew_ref[pl.ds(at, SUB, stride=SUB), :] = pltpu.roll(block, s, 1) if s else block
-
-
 def frame_of(code, period, all_ref):
     return all_ref[code >> CODE_BITS, SUB : 2 * SUB, :] + offset_rows(code, period, all_ref.shape[2])
 
 
-def near_blocks(own_frame, partner_frame):
+def lanes_of(block, member):
+    row = lax.broadcasted_iota(jnp.int32, (SUB, member), 0)
+    lane = lax.broadcasted_iota(jnp.int32, (SUB, member), 1)
+    group = (lane & -LAYER) - (block >> 1) * LAYER
+    return (group & (member - 1)) + ((block & 1) * SUB + row)
+
+
+def picked(block, lanes):
+    return jnp.take_along_axis(block, lanes, axis=1, mode="promise_in_bounds")
+
+
+def near_blocks(own_frame, partner_frame, box_lanes_ref):
     member = own_frame.shape[1]
     row = lax.broadcasted_iota(jnp.int32, (SUB, member), 0)
     sign = jnp.where(row < 3, 1.0, jnp.where(row < 6, -1.0, 0.0))
@@ -168,12 +174,12 @@
 
     box = doubled(partner_frame) * sign
     for bit in (1, 2, 4):
-        box = jnp.maximum(box, pltpu.roll(box, bit, 1))
+        box = jnp.maximum(box, pltpu.roll(box, member - bit, 1))
     here = doubled(own_frame) * sign
     blocks = member // SUB
     reach = []
     for k in range(blocks):
-        gap = jnp.maximum(here - (pltpu.roll(box, k * SUB, 1) if k else box), 0.0)
+        gap = jnp.maximum(here - picked(box, box_lanes_ref[k * SUB : (k + 1) * SUB, :]), 0.0)
         reach.append(jnp.sum(gap * gap, axis=0, keepdims=True))
     nearest = jnp.min(jnp.concatenate(reach, axis=0), axis=1, keepdims=True)
     weight = (1 << lax.broadcasted_iota(jnp.int32, (blocks, 1), 0)).astype(jnp.float32)
@@ -188,37 +194,48 @@
     return jnp.broadcast_to(block[k : k + 1], (GROUP * SUB, block.shape[1]))
 
 
-def turned(skew_ref, items, k):
-    parts = []
-    for item in items:
-        start = pl.multiple_of((item >> ITEM_BITS) * (SUB * SUB) + k * SUB, SUB)
-        parts.append(pltpu.roll(skew_ref[pl.ds(start, SUB), :], item & ITEM_MASK, 1))
-    return stacked(parts)
+def partner_rows(tiles_ref, items, lanes, first):
+    member = tiles_ref.shape[2]
+    rows = []
+    for k in range(6):
+        parts = []
+        for item, lane in zip(items, lanes):
+            row = tiles_ref[item >> (ITEM_BITS + CODE_BITS), first + k : first + k + 1, :]
+            parts.append(picked(jnp.broadcast_to(row, (SUB, member)), lane))
+        rows.append(stacked(parts))
+    return rows
 
 
 def folded(total):
     return jnp.sum(total, axis=0, keepdims=True)
 
 
-def geometry(items, unused, own_wide, skew_ref):
-    member = skew_ref.shape[1]
-    first_row = (lax.broadcasted_iota(jnp.int32, (SUB, member), 0) == 0).astype(jnp.float32)
-    itself = [jnp.where(item == 0, 2.0 * cutoff_sq, 0.0) for item in items]
-    lift = stacked([first_row * one + jnp.where(two, 2.0 * cutoff_sq, 0.0) for one, two in zip(itself, unused)])
-    d = [turned(skew_ref, items, k) - own_wide[k] for k in range(3)]
-    uj = [turned(skew_ref, items, 3 + k) for k in range(3)]
-    gradient, hessian, spin = pair_coefficients(d, own_wide[3:], uj, lift)
+def geometry(items, unused, lanes, own_code, own_wide, period, all_ref):
+    member = all_ref.shape[2]
+    lane = lax.broadcasted_iota(jnp.int32, (SUB, member), 1)
+    lift = []
+    shifts = []
+    for item, idle, other in zip(items, unused, lanes):
+        code = item >> ITEM_BITS
+        itself = jnp.where(other == lane, jnp.where(code == own_code, 2.0 * cutoff_sq, 0.0), 0.0)
+        lift.append(itself + jnp.where(idle, 2.0 * cutoff_sq, 0.0))
+        shifts.append(offsets_of(code, period))
+    rows = partner_rows(all_ref, items, lanes, SUB)
+    shift = [stacked([jnp.full((SUB, member), one[k]) for one in shifts]) for k in range(3)]
+    d = [rows[k] + shift[k] - own_wide[k] for k in range(3)]
+    uj = rows[3:]
+    gradient, hessian, spin = pair_coefficients(d, own_wide[3:], uj, stacked(lift))
     return list(gradient) + list(hessian) + d + uj, (gradient[1], spin)
 
 
-def apply(items, terms, own_wide, moved_wide, skew_ref):
+def apply(moved_rows, terms, own_wide, moved_wide):
     u_e, u_a, u_b, u_c, h_ee, h_ea, h_eb, h_ec, h_aa, h_ab, h_ac, h_bb, h_bc, h_cc = terms[:14]
     d = terms[14:17]
     uj = terms[17:20]
     ui = own_wide[3:]
     dui = moved_wide[3:]
-    dd = [turned(skew_ref, items, k) - moved_wide[k] for k in range(3)]
-    duj = [turned(skew_ref, items, 3 + k) for k in range(3)]
+    dd = [moved_rows[k] - moved_wide[k] for k in range(3)]
+    duj = moved_rows[3:]
     de = dot3(d, dd)
     da = dot3(dd, ui) + dot3(d, dui)
     db = dot3(dd, uj) + dot3(d, duj)
@@ -274,13 +291,12 @@
     period,
     all_ref,
     out_ref,
-    entry_ref,
     item_ref,
     count_ref,
     coef_ref,
     kept_ref,
-    skew_ref,
-    frame_skew_ref,
+    entry_ref,
+    box_lanes_ref,
     code_ref,
     code_smem,
     sem,
@@ -311,9 +327,12 @@
         code_ref[cols + row : cols + row + 1, :] = jnp.where(hit, code, -1.0).astype(jnp.int32)
     copy = pltpu.make_async_copy(code_ref, code_smem, sem)
     copy.start()
+    for block in range(blocks):
+        box_lanes_ref[block * SUB : (block + 1) * SUB, :] = lanes_of(block, member) & -SUB
     copy.wait()
 
-    entry_ref[0] = own * (1 << CODE_BITS) + 21
+    own_code = own * (1 << CODE_BITS) + 21
+    entry_ref[0] = own_code
 
     def gather(line, count):
         for slot in range(slots):
@@ -329,19 +348,16 @@
     def prepare(entry, count):
         code = entry_ref[entry]
         frame = frame_of(code, period, all_ref)
-        skew_entry(entry, frame, frame_skew_ref)
-        skew_entry(entry, all_ref[code >> CODE_BITS, 0:SUB, :], skew_ref)
-        bits = near_blocks(own_frame, frame)
+        bits = near_blocks(own_frame, frame, box_lanes_ref)
         for block in range(blocks):
-            item_ref[count] = (entry << ITEM_BITS) + block * SUB
+            item_ref[count] = (code << ITEM_BITS) + block
             count = count + (bits >> block & 1)
         return count
 
     items = lax.fori_loop(0, entries, prepare, jnp.int32(0))
     for part in range(GROUP):
-        item_ref[items + part] = 0
-    count_ref[0] = entries
-    count_ref[1] = items
+        item_ref[items + part] = own_code << ITEM_BITS
+    count_ref[0] = items
 
     held = coef_ref.shape[0] // (TERMS * GROUP * SUB)
     steps = (items + GROUP - 1) // GROUP
@@ -350,8 +366,10 @@
 
     def derive(step, totals):
         group, unused = group_items(step, item_ref, items)
-        terms, sums = geometry(group, unused, own_wide, frame_skew_ref)
-        return terms, added(totals, apply(group, terms, own_wide, moved_wide, skew_ref) + list(sums))
+        lanes = [lanes_of(item & ITEM_MASK, member) for item in group]
+        terms, sums = geometry(group, unused, lanes, own_code, own_wide, period, all_ref)
+        moved_rows = partner_rows(all_ref, group, lanes, 0)
+        return terms, added(totals, apply(moved_rows, terms, own_wide, moved_wide) + list(sums))
 
     def keep(step, totals):
         terms, totals = derive(step, totals)
@@ -381,7 +399,6 @@
     cols,
     total_entries,
     period,
-    entry_ref,
     item_ref,
     count_ref,
     coef_ref,
@@ -393,8 +410,6 @@
     scalar_ref,
     basis_ref,
     second_ref,
-    skew_ref,
-    frame_skew_ref,
 ):
     own = lax.axis_index("row") * cols + lax.axis_index("col")
     member = all_ref.shape[2]
@@ -405,23 +420,10 @@
     beta = jnp.sqrt(whole_sum(second_ref, second_ref) / total_entries / norm_sq + norm_eps)
     scale = lax.rsqrt(norm_sq) / beta
 
-    entries = count_ref[0]
-    items = count_ref[1]
+    own_code = own * (1 << CODE_BITS) + 21
+    items = count_ref[0]
     held = coef_ref.shape[0] // (TERMS * GROUP * SUB)
     steps = (items + GROUP - 1) // GROUP
-
-    def prepare(entry, carry):
-        skew_entry(entry, second_ref[entry_ref[entry] >> CODE_BITS], skew_ref)
-        return carry
-
-    lax.fori_loop(0, entries, prepare, 0)
-
-    def prepare_frame(entry, carry):
-        skew_entry(entry, frame_of(entry_ref[entry], period, all_ref), frame_skew_ref)
-        return carry
-
-    lax.fori_loop(0, jnp.where(steps > held, entries, 0), prepare_frame, 0)
-
     own_frame = all_ref[own, SUB : 2 * SUB, :]
     own_moved = second_ref[own]
     own_wide = [wide(own_frame, k) for k in range(6)]
@@ -429,14 +431,16 @@
 
     def visit(step, totals):
         group, _ = group_items(step, item_ref, items)
+        lanes = [lanes_of(item & ITEM_MASK, member) for item in group]
         start = pl.multiple_of(step * (TERMS * GROUP * SUB), SUB)
         terms = [coef_ref[pl.ds(start + k * GROUP * SUB, GROUP * SUB), :] for k in range(TERMS)]
-        return added(totals, apply(group, terms, own_wide, moved_wide, skew_ref))
+        return added(totals, apply(partner_rows(second_ref, group, lanes, 0), terms, own_wide, moved_wide))
 
     def visit_again(step, totals):
         group, unused = group_items(step, item_ref, items)
-        terms, _ = geometry(group, unused, own_wide, frame_skew_ref)
-        return added(totals, apply(group, terms, own_wide, moved_wide, skew_ref))
+        lanes = [lanes_of(item & ITEM_MASK, member) for item in group]
+        terms, _ = geometry(group, unused, lanes, own_code, own_wide, period, all_ref)
+        return added(totals, apply(partner_rows(second_ref, group, lanes, 0), terms, own_wide, moved_wide))
 
     zero = jnp.zeros((SUB, member), jnp.float32)
     totals = lax.fori_loop(0, jnp.minimum(steps, held), visit, (zero,) * 7)
@@ -511,23 +515,21 @@
     )(config, start, list_row)
     together = everywhere(packed)
 
-    skew = pltpu.VMEM((longest * SUB * SUB, member), jnp.float32)
     held_rows = HELD // GROUP * (TERMS * GROUP * SUB)
-    image, codes, items, counts, terms, kept = pl.pallas_call(
+    image, items, counts, terms, kept = pl.pallas_call(
         functools.partial(first_kernel, row_devices, col_devices, slots, period),
         out_shape=(
             shaped(devices, SUB, member),
-            jax.ShapeDtypeStruct((longest + 1,), jnp.int32),
             jax.ShapeDtypeStruct((longest * (member // SUB) + GROUP,), jnp.int32),
-            jax.ShapeDtypeStruct((2,), jnp.int32),
+            jax.ShapeDtypeStruct((1,), jnp.int32),
             shaped(held_rows, member),
             shaped(2, member),
         ),
         in_specs=[vmem],
-        out_specs=(vmem, smem, smem, smem, vmem, vmem),
+        out_specs=(vmem, smem, smem, vmem, vmem),
         scratch_shapes=[
-            skew,
-            skew,
+            pltpu.SMEM((longest + 1,), jnp.int32),
+            pltpu.VMEM((member, member), jnp.int32),
             pltpu.VMEM((row_devices + col_devices, member), jnp.int32),
             pltpu.SMEM((row_devices + col_devices, member), jnp.int32),
             pltpu.SemaphoreType.DMA,
@@ -539,16 +541,14 @@
     line, pair, scalars = pl.pallas_call(
         functools.partial(second_kernel, col_devices, total_entries, period),
         out_shape=(shaped(devices, 1, member), shaped(2, SUB, member), shaped(1, member)),
-        in_specs=[smem] * 3 + [vmem] * 4,
+        in_specs=[smem] * 2 + [vmem] * 4,
         out_specs=(vmem, vmem, vmem),
         scratch_shapes=[
             pltpu.VMEM((devices, SUB, member), jnp.float32),
             pltpu.VMEM((devices, SUB, member), jnp.float32),
-            skew,
-            skew,
         ],
         compiler_params=params,
-    )(codes, items, counts, terms, kept, together, image)
+    )(items, counts, terms, kept, together, image)
     line = everywhere(line)
 
     mode, coefficients = pl.pallas_call(

time: 62.9 us -> 56.5 us (0.90); the launches traced: 62.8 us -> 55.7 us
  blocking collectives: 47.6 us -> 40.6 us
    all_to_all x3, blocking collectives: 47.6 us -> 40.6 us  [everywhere(): return lax.all_to_all(copies, ('row', 'col'), 0, 0, tiled=True)]
where the time goes in v2:
time: 56.5 us; the launch traced here: 55.7 us
  blocking collectives  40.6 us (72%)
  Pallas kernels  10.8 us (19%)
  local copies, waits for them, and re-layouts  2.82 us (5%)
  between operations  1.33 us (2%)
    all_to_all x3, blocking collectives, everywhere(): return lax.all_to_all(copies, ('row', 'col'), 0, 0, tiled=True)  40.6 us
    pallas_call x1, Pallas kernels, local(): pl.pallas_call(functools.partial(first_kernel, row_devices, col_devices,...  7.36 us
    pallas_call x1, Pallas kernels, local(): pl.pallas_call(functools.partial(second_kernel, col_devices, total_entrie...  2.65 us
    unnamed x7, local copies, waits for them, and re-layouts  2.14 us

profile of v2, /device:TPU:0, one launch (start us, length us, event | category | flops | bytes accessed | tf_op | source)
XLA Modules:
  0.0 55.7 jit_solution(9028950584899075873)
XLA Ops:
  0.6 0.0 copy-start.1
  1.3 0.8 %copy.6 = s32[1,1,8,5]{3,2,1,0:T(8,128)S(1)} copy(s32[1,1,8,5]{2,1,3,0:T(1,128)} %param.6) | data formatting | bytes 320 | tf_op args[2]
  2.1 0.1 fusion.1
  2.1 0.1 copy.7
  2.2 0.1 reshape.11
  2.3 0.0 copy-start
  2.3 0.7 %copy-done = f32[6,128]{1,0:T(8,128)S(1)} copy-done((f32[6,128]{1,0:T(8,128)S(1)}, f32[6,128]{1,0:T(8,128)}, u32[]{:S(2)}) %copy-start) | copy-done | bytes 3096
  3.0 0.0 copy-start.2
  3.0 0.7 %copy-done.2 = f32[6,128]{1,0:T(8,128)S(1)} copy-done((f32[6,128]{1,0:T(8,128)S(1)}, f32[6,128]{1,0:T(8,128)}, u32[]{:S(2)}) %copy-start.2) | copy-done | bytes 3096
  3.7 17.7 %all_to_all.15.all_ref = f32[32,16,128]{2,1,0:T(8,128)S(1)} all-to-all(f32[32,16,128]{2,1,0:T(8,128)S(1)} %shard_map.59), channel_id=1, replica_groups=mesh['row'=4,'col'=8] {'row','col'}, dimensions={0} | all-to-all | bytes 524288 | tf_op jit(solution)/shard_map/all_to_all | solution.py:499
  21.4 7.4 %shard_map.60 = (f32[32,8,128]{2,1,0:T(8,128)S(1)}, s32[1554]{0:T(1024)S(1)}, s32[1]{0:T(128)}, f32[20480,128]{1,0:T(8,128)S(1)}, f32[2,128]{1,0:T(2,128)S(1)}) custom-call(f32[32,16,128]{2,1,0:T(8,128)S(1)} %all_to_all.15.all_ref), custom_call_target="tpu_custom_call" | custom-call | tf_op jit(solution)/shard_map/pallas_call | solution.py:519
  28.8 13.3 %all_to_all.16.image_ref = f32[32,8,128]{2,1,0:T(8,128)S(1)} all-to-all(f32[32,8,128]{2,1,0:T(8,128)S(1)} %get-tuple-element.16), channel_id=1, replica_groups=mesh['row'=4,'col'=8] {'row','col'}, dimensions={0} | all-to-all | bytes 262144 | tf_op jit(solution)/shard_map/all_to_all | solution.py:499
  42.1 2.6 %shard_map.61 = (f32[32,1,128]{2,1,0:T(1,128)S(1)}, f32[2,8,128]{2,1,0:T(8,128)S(1)}, f32[1,128]{1,0:T(1,128)S(1)}) custom-call(s32[1554]{0:T(1024)S(1)} %get-tuple-element.12.item_ref, s32[1]{0:T(128)} %get-tuple-element.13.count_ref, f32[20480,128]{1,0:T(8,128)S(1)} %get-tuple-element.14.coef_ref, f32[2,128]{1,0:T(2,128)S(1)} %get-tuple-element.15.kept_ref, ...), custom_call_target="tpu_custom_call" | custom-call | tf_op jit(solution)/shard_map/pallas_call | solution.py:541
  44.7 9.6 %all_to_all.17.line_ref = f32[32,1,128]{2,1,0:T(1,128)S(1)} all-to-all(f32[32,1,128]{2,1,0:T(1,128)S(1)} %get-tuple-element.19), channel_id=1, replica_groups=mesh['row'=4,'col'=8] {'row','col'}, dimensions={0} | all-to-all | bytes 32768 | tf_op jit(solution)/shard_map/all_to_all | solution.py:499
  54.4 0.0 copy-done.1
  54.4 0.8 %shard_map.62 = (f32[6,128]{1,0:T(8,128)}, f32[1,128]{1,0:T(1,128)S(1)}) custom-call(f32[6,128]{1,0:T(8,128)S(1)} %copy-done.1, f32[2,8,128]{2,1,0:T(8,128)S(1)} %get-tuple-element.17.pair_ref, f32[1,128]{1,0:T(1,128)S(1)} %get-tuple-element.18.scalar_ref, f32[32,1,128]{2,1,0:T(1,128)S(1)} %all_to_all.17.line_ref), custom_call_target="tpu_custom_call" | custom-call | tf_op jit(solution)/shard_map/pallas_call | solution.py:554
  55.2 0.5 slice_bitcast_fusion
  (3 shorter events, 0.0 us)
Async XLA Ops:
  0.6 53.8 %copy-start.1 = (f32[6,128]{1,0:T(8,128)S(1)}, f32[6,128]{1,0:T(8,128)}, u32[]{:S(2)}) copy-start(f32[6,128]{1,0:T(8,128)} %config_ref.3) | copy-start | bytes 9220
  2.3 0.7 %copy-start = (f32[6,128]{1,0:T(8,128)S(1)}, f32[6,128]{1,0:T(8,128)}, u32[]{:S(2)}) copy-start(f32[6,128]{1,0:T(8,128)} %config_ref.3) | copy-start | bytes 9220
  3.0 0.7 %copy-start.2 = (f32[6,128]{1,0:T(8,128)S(1)}, f32[6,128]{1,0:T(8,128)}, u32[]{:S(2)}) copy-start(f32[6,128]{1,0:T(8,128)} %start_ref.1) | copy-start | bytes 9220

commit v3 on v2

--- a/solution.py
+++ b/solution.py
@@ -20,10 +20,12 @@
 ITEM_BITS = 8
 ITEM_MASK = 255
 LAYER = 16
+TESTS = 4
 GROUP = 2
 TERMS = 20
 HELD = 128
 VMEM_LIMIT = 32 * 1024 * 1024
+PACK_LIMIT = 60 * 1024 * 1024
 
 
 def dot3(a, b):
@@ -163,25 +165,31 @@
     return jnp.take_along_axis(block, lanes, axis=1, mode="promise_in_bounds")
 
 
-def near_blocks(own_frame, partner_frame, box_lanes_ref):
-    member = own_frame.shape[1]
+def box_lanes(member):
+    block = lax.broadcasted_iota(jnp.int32, (member // SUB, member), 0)
+    lane = lax.broadcasted_iota(jnp.int32, (member // SUB, member), 1)
+    return (((lane & -LAYER) - (block >> 1) * LAYER) & (member - 1)) + (block & 1) * SUB
+
+
+def near_blocks(own_centre, partner_frame, lanes):
+    blocks, member = lanes.shape
     row = lax.broadcasted_iota(jnp.int32, (SUB, member), 0)
-    sign = jnp.where(row < 3, 1.0, jnp.where(row < 6, -1.0, 0.0))
-
-    def doubled(block):
-        centre = jnp.where(row < 3, block, 0.0)
-        return centre + pltpu.roll(centre, 3, 0)
-
-    box = doubled(partner_frame) * sign
+    centre = jnp.where(row < 3, partner_frame, 0.0)
+    box = centre - pltpu.roll(centre, 3, 0)
     for bit in (1, 2, 4):
         box = jnp.maximum(box, pltpu.roll(box, member - bit, 1))
-    here = doubled(own_frame) * sign
-    blocks = member // SUB
-    reach = []
-    for k in range(blocks):
-        gap = jnp.maximum(here - picked(box, box_lanes_ref[k * SUB : (k + 1) * SUB, :]), 0.0)
-        reach.append(jnp.sum(gap * gap, axis=0, keepdims=True))
-    nearest = jnp.min(jnp.concatenate(reach, axis=0), axis=1, keepdims=True)
+
+    def seen(k):
+        line = jnp.broadcast_to(box[k : k + 1], (SUB, member))
+        return stacked([picked(line, lanes[at : at + SUB]) for at in range(0, blocks, SUB)])
+
+    reach = 0.0
+    for k in range(3):
+        above = own_centre[k] - seen(k)
+        below = -own_centre[k] - seen(3 + k)
+        gap = jnp.maximum(jnp.maximum(above, below), 0.0)
+        reach = reach + gap * gap
+    nearest = jnp.min(reach, axis=1, keepdims=True)
     weight = (1 << lax.broadcasted_iota(jnp.int32, (blocks, 1), 0)).astype(jnp.float32)
     return jnp.sum(jnp.where(nearest < cutoff_sq * 1.001, weight, 0.0)).astype(jnp.int32)
 
@@ -276,12 +284,30 @@
     out_ref[...] = jnp.broadcast_to(block[None], out_ref.shape)
 
 
-def pack_kernel(config_ref, start_ref, list_ref, out_ref):
+def pack_kernel(*refs):
+    sources, out_ref, targets, sems = refs[:4], refs[4], refs[5:9], refs[9]
+    config_ref, start_ref, list_ref, count_ref = targets
     member = out_ref.shape[2]
+    copies = [
+        pltpu.make_async_copy(source, target, sems.at[at]) for at, (source, target) in enumerate(zip(sources, targets))
+    ]
+    for copy in copies:
+        copy.start()
+    copies[2].wait()
+    copies[3].wait()
+    lane = lax.broadcasted_iota(jnp.int32, (1, member), 1)
+    fields, slots = list_ref.shape[1], list_ref.shape[3]
+    line = jnp.full((1, member), -9, jnp.int32)
+    for field in range(fields):
+        for slot in range(slots):
+            line = jnp.where(lane == field * slots + slot, list_ref[0, field, 0, slot], line)
+    line = jnp.where((lane >= count_ref[0, 0]) & (lane < slots), -9, line).astype(jnp.float32)
+    copies[0].wait()
+    copies[1].wait()
     u = [config_ref[k : k + 1, :] for k in range(3, 6)]
     w = [start_ref[k : k + 1, :] for k in range(3, 6)]
     zero = jnp.zeros((1, member), jnp.float32)
-    spread([start_ref[0:3, :], *cross3(w, u), dot3(w, u), zero, config_ref[...], list_ref[...], zero], out_ref)
+    spread([start_ref[0:3, :], *cross3(w, u), dot3(w, u), zero, config_ref[...], line, zero], out_ref)
 
 
 def first_kernel(
@@ -296,7 +322,6 @@
     coef_ref,
     kept_ref,
     entry_ref,
-    box_lanes_ref,
     code_ref,
     code_smem,
     sem,
@@ -310,29 +335,35 @@
     def field(line, at):
         return line if at == 0 else pltpu.roll(line, member - at * slots, 1)
 
-    def encode(line, partner, side):
-        offset = (field(line, 2) * 16.0 + field(line, 3) * 4.0 + field(line, 4)) * side + 21.0
-        return partner * float(1 << CODE_BITS) + offset
-
     row_f = row_id.astype(jnp.float32)
     col_f = col_id.astype(jnp.float32)
-    for col in range(cols):
-        line = all_ref[row_id * cols + col, LIST_ROW : LIST_ROW + 1, :]
-        code = encode(line, field(line, 1) * float(cols) + float(col), 1.0)
-        code_ref[col : col + 1, :] = jnp.where(line == col_f, code, -1.0).astype(jnp.int32)
-    for row in range(rows):
-        line = all_ref[row * cols + col_id, LIST_ROW : LIST_ROW + 1, :]
-        code = encode(line, float(row * cols) + line, -1.0)
-        hit = (field(line, 1) == row_f) & (line >= 0.0)
-        code_ref[cols + row : cols + row + 1, :] = jnp.where(hit, code, -1.0).astype(jnp.int32)
+    lines = [all_ref[row_id * cols + col, LIST_ROW : LIST_ROW + 1, :] for col in range(cols)]
+    lines += [all_ref[row * cols + col_id, LIST_ROW : LIST_ROW + 1, :] for row in range(rows)]
+    line = jnp.concatenate(lines, axis=0)
+    at = lax.broadcasted_iota(jnp.int32, line.shape, 0).astype(jnp.float32)
+    near = at < float(cols)
+    other = field(line, 1)
+    offset = field(line, 2) * 16.0 + field(line, 3) * 4.0 + field(line, 4)
+    partner = jnp.where(near, other * float(cols) + at, (at - float(cols)) * float(cols) + line)
+    code = partner * float(1 << CODE_BITS) + (jnp.where(near, offset, -offset) + 21.0)
+    hit = jnp.where(near, line - col_f, jnp.where(line >= 0.0, other - row_f, 1.0)) == 0.0
+    code_ref[...] = jnp.where(hit, code, -1.0).astype(jnp.int32)
     copy = pltpu.make_async_copy(code_ref, code_smem, sem)
     copy.start()
-    for block in range(blocks):
-        box_lanes_ref[block * SUB : (block + 1) * SUB, :] = lanes_of(block, member) & -SUB
+    own_code = own * (1 << CODE_BITS) + 21
+    own_frame = all_ref[own, SUB : 2 * SUB, :]
+    own_moved = all_ref[own, 0:SUB, :]
+    lanes = box_lanes(member)
+    own_centre = [jnp.broadcast_to(own_frame[k : k + 1], lanes.shape) for k in range(3)]
+
+    def append(code, bits, count):
+        for block in range(blocks):
+            item_ref[count] = (code << ITEM_BITS) + block
+            count = count + (bits >> block & 1)
+        return count
+
+    items = append(own_code, near_blocks(own_centre, own_frame, lanes), jnp.int32(0))
     copy.wait()
-
-    own_code = own * (1 << CODE_BITS) + 21
-    entry_ref[0] = own_code
 
     def gather(line, count):
         for slot in range(slots):
@@ -341,20 +372,18 @@
             count = count + (code >= 0).astype(jnp.int32)
         return count
 
-    entries = lax.fori_loop(0, rows + cols, gather, jnp.int32(1))
-    own_frame = all_ref[own, SUB : 2 * SUB, :]
-    own_moved = all_ref[own, 0:SUB, :]
-
-    def prepare(entry, count):
-        code = entry_ref[entry]
-        frame = frame_of(code, period, all_ref)
-        bits = near_blocks(own_frame, frame, box_lanes_ref)
-        for block in range(blocks):
-            item_ref[count] = (code << ITEM_BITS) + block
-            count = count + (bits >> block & 1)
+    entries = lax.fori_loop(0, rows + cols, gather, jnp.int32(0))
+    for part in range(TESTS):
+        entry_ref[entries + part] = own_code
+
+    def prepare(step, count):
+        codes = [entry_ref[step * TESTS + part] for part in range(TESTS)]
+        bits = [near_blocks(own_centre, frame_of(code, period, all_ref), lanes) for code in codes]
+        for part in range(TESTS):
+            count = append(codes[part], jnp.where(step * TESTS + part < entries, bits[part], 0), count)
         return count
 
-    items = lax.fori_loop(0, entries, prepare, jnp.int32(0))
+    items = lax.fori_loop(0, (entries + TESTS - 1) // TESTS, prepare, items)
     for part in range(GROUP):
         item_ref[items + part] = own_code << ITEM_BITS
     count_ref[0] = items
@@ -384,11 +413,6 @@
     sums = [folded(total) for total in totals]
     kept_ref[...] = jnp.concatenate(sums[7:], axis=0)
     spread(close(sums, sums[7], sums[8], own_frame, own_moved), out_ref)
-
-
-def whole_sum(left_ref, right_ref):
-    total = jnp.sum(left_ref[...] * right_ref[...], axis=0)
-    return jnp.sum(jnp.sum(total, axis=0, keepdims=True), axis=1, keepdims=True)
 
 
 def scalar_of(block):
@@ -408,17 +432,20 @@
     out_ref,
     pair_ref,
     scalar_ref,
-    basis_ref,
     second_ref,
 ):
     own = lax.axis_index("row") * cols + lax.axis_index("col")
     member = all_ref.shape[2]
-    basis_ref[...] = all_ref[:, 0:SUB, :]
-    norm_sq = whole_sum(basis_ref, basis_ref) / total_entries + norm_eps
-    alpha = whole_sum(basis_ref, image_ref) / total_entries / norm_sq
-    second_ref[...] = image_ref[...] - alpha * basis_ref[...]
-    beta = jnp.sqrt(whole_sum(second_ref, second_ref) / total_entries / norm_sq + norm_eps)
-    scale = lax.rsqrt(norm_sq) / beta
+    basis = all_ref[:, 0:SUB, :]
+    portion = 1.0 / total_entries
+    norm_sq = scalar_of(jnp.sum(basis * basis, axis=0)) * portion + norm_eps
+    norm_inv = lax.rsqrt(norm_sq)
+    alpha = scalar_of(jnp.sum(basis * image_ref[...], axis=0)) * portion / norm_sq
+    second = image_ref[...] - alpha * basis
+    second_ref[...] = second
+    beta_sq = scalar_of(jnp.sum(second * second, axis=0)) * portion / norm_sq + norm_eps
+    beta = jnp.sqrt(beta_sq)
+    scale = norm_inv * lax.rsqrt(beta_sq)
 
     own_code = own * (1 << CODE_BITS) + 21
     items = count_ref[0]
@@ -448,7 +475,7 @@
     sums = [folded(total) for total in totals]
     product = close(sums, kept_ref[0:1, :], kept_ref[1:2, :], own_frame, own_moved)
     fill = [jnp.zeros((1, member), jnp.float32)] * (SUB - len(product))
-    image = jnp.concatenate(product + fill, axis=0) * scale - (beta * lax.rsqrt(norm_sq)) * basis_ref[own]
+    image = jnp.concatenate(product + fill, axis=0) * scale - (beta * norm_inv) * all_ref[own, 0:SUB, :]
     second = second_ref[own] * scale
     inner = scalar_of(second * image)
     weight = scalar_of(second * second)
@@ -477,8 +504,8 @@
     turn = cross3(u, [mine[k : k + 1] for k in range(3, 6)])
     along = mine[6:7]
     mode_ref[...] = jnp.concatenate([mine[0:3]] + [turn[k] + along * u[k] for k in range(3)], axis=0)
-    lane = lax.broadcasted_iota(jnp.int32, scalar_ref.shape, 1)
-    coefficient_ref[...] = jnp.where(lane == 2, alpha, jnp.where(lane == 3, beta, scalar_ref[...]))
+    for at, value in enumerate((scalar_ref[0:1, 0:1], scalar_ref[0:1, 1:2], alpha, beta)):
+        coefficient_ref[at] = jnp.sum(value)
 
 
 def local(config, start, tile_list, tile_count):
@@ -488,8 +515,7 @@
     devices = row_devices * col_devices
     total_entries = float(dof * member * devices)
     period = (5.0, 5.0, 3.5 * (member // 16))
-    entries = tile_list[0, 0]
-    slots, fields = entries.shape
+    slots = tile_list.shape[2]
     longest = (row_devices + col_devices) * slots + 1
 
     def shaped(*shape):
@@ -502,17 +528,21 @@
     vmem = pl.BlockSpec(memory_space=pltpu.VMEM)
     smem = pl.BlockSpec(memory_space=pltpu.SMEM)
 
-    in_use = jnp.arange(slots, dtype=jnp.int32) < tile_count[0, 0]
-    fields_f = jnp.where(in_use[:, None], entries, -9).astype(jnp.float32).T.reshape(1, fields * slots)
-    list_row = jnp.pad(fields_f, ((0, 0), (0, member - fields * slots)), constant_values=-9.0)
-
+    outside = pl.BlockSpec(memory_space=pl.ANY)
     packed = pl.pallas_call(
         pack_kernel,
         out_shape=shaped(devices, 2 * SUB, member),
-        in_specs=[vmem] * 3,
+        in_specs=[outside] * 4,
         out_specs=vmem,
-        compiler_params=params,
-    )(config, start, list_row)
+        scratch_shapes=[
+            pltpu.VMEM((dof, member), jnp.float32),
+            pltpu.VMEM((dof, member), jnp.float32),
+            pltpu.SMEM((1, tile_list.shape[3], 1, slots), jnp.int32),
+            pltpu.SMEM((1, 1), jnp.int32),
+            pltpu.SemaphoreType.DMA((4,)),
+        ],
+        compiler_params=pltpu.CompilerParams(vmem_limit_bytes=PACK_LIMIT),
+    )(config, start, jnp.transpose(tile_list, (0, 3, 1, 2)), tile_count)
     together = everywhere(packed)
 
     held_rows = HELD // GROUP * (TERMS * GROUP * SUB)
@@ -528,8 +558,7 @@
         in_specs=[vmem],
         out_specs=(vmem, smem, smem, vmem, vmem),
         scratch_shapes=[
-            pltpu.SMEM((longest + 1,), jnp.int32),
-            pltpu.VMEM((member, member), jnp.int32),
+            pltpu.SMEM((longest + TESTS,), jnp.int32),
             pltpu.VMEM((row_devices + col_devices, member), jnp.int32),
             pltpu.SMEM((row_devices + col_devices, member), jnp.int32),
             pltpu.SemaphoreType.DMA,
@@ -545,7 +574,6 @@
         out_specs=(vmem, vmem, vmem),
         scratch_shapes=[
             pltpu.VMEM((devices, SUB, member), jnp.float32),
-            pltpu.VMEM((devices, SUB, member), jnp.float32),
         ],
         compiler_params=params,
     )(items, counts, terms, kept, together, image)
@@ -553,12 +581,12 @@
 
     mode, coefficients = pl.pallas_call(
         functools.partial(last_kernel, total_entries),
-        out_shape=(shaped(dof, member), shaped(1, member)),
+        out_shape=(shaped(dof, member), shaped(4)),
         in_specs=[vmem] * 4,
-        out_specs=(vmem, vmem),
+        out_specs=(vmem, smem),
         compiler_params=params,
     )(config, pair, scalars, line)
-    return (coefficients[0, :4], mode)
+    return (coefficients, mode)
 
 
 def solution(mesh):

time: 56.5 us -> 49.7 us (0.88); the launches traced: 55.7 us -> 49.6 us
  local copies, waits for them, and re-layouts: 2.82 us -> 0.01 us
  Pallas kernels: 10.8 us -> 8.54 us
  blocking collectives: 40.6 us -> 39.8 us
    pallas_call x1, Pallas kernels: 7.36 us -> 3.81 us  [local(): pl.pallas_call(functools.partial(first_kernel, row_devices, col_devices,...]
    unnamed x7 -> x2, local copies, waits for them, and re-layouts: 2.14 us -> 0.01 us
    pallas_call x1, Pallas kernels: 0.02 us -> 1.61 us  [local(): pl.pallas_call(pack_kernel, out_shape=shaped(devices, 2 * SUB, member), i...]
    all_to_all x3, blocking collectives: 40.6 us -> 39.8 us  [everywhere(): return lax.all_to_all(copies, ('row', 'col'), 0, 0, tiled=True)]
where the time goes in v3:
time: 49.7 us; the launch traced here: 49.6 us
  blocking collectives  39.8 us (80%)
  Pallas kernels  8.54 us (17%)
  between operations  1.32 us (3%)
    all_to_all x3, blocking collectives, everywhere(): return lax.all_to_all(copies, ('row', 'col'), 0, 0, tiled=True)  39.8 us
    pallas_call x1, Pallas kernels, local(): pl.pallas_call(functools.partial(first_kernel, row_devices, col_devices,...  3.81 us
    pallas_call x1, Pallas kernels, local(): pl.pallas_call(functools.partial(second_kernel, col_devices, total_entrie...  2.31 us
    pallas_call x1, Pallas kernels, local(): pl.pallas_call(pack_kernel, out_shape=shaped(devices, 2 * SUB, member), i...  1.61 us

profile of v3, /device:TPU:0, one launch (start us, length us, event | category | flops | bytes accessed | tf_op | source)
XLA Modules:
  0.0 49.6 jit_solution(738502237721451385)
XLA Ops:
  0.6 0.0 copy-start
  1.3 1.6 %shard_map.59 = f32[32,16,128]{2,1,0:T(8,128)} custom-call(f32[6,128]{1,0:T(8,128)} %config_ref.1, f32[6,128]{1,0:T(8,128)} %refs_1_.1, s32[1,5,1,8]{3,2,1,0:T(1,128)} %bitcast.1, s32[1,1]{1,0:T(1,128)S(6)} %copy.6.refs_3_), custom_call_target="tpu_custom_call" | custom-call | tf_op jit(solution)/shard_map/pallas_call | solution.py:532
  2.9 17.9 %all_to_all.15.all_ref = f32[32,16,128]{2,1,0:T(8,128)S(1)} all-to-all(f32[32,16,128]{2,1,0:T(8,128)} %shard_map.59), channel_id=1, replica_groups=mesh['row'=4,'col'=8] {'row','col'}, dimensions={0} | all-to-all | bytes 524288 | tf_op jit(solution)/shard_map/all_to_all | solution.py:525
  20.8 3.8 %shard_map.60 = (f32[32,8,128]{2,1,0:T(8,128)S(1)}, s32[1554]{0:T(1024)S(1)}, s32[1]{0:T(128)}, f32[20480,128]{1,0:T(8,128)S(1)}, f32[2,128]{1,0:T(2,128)S(1)}) custom-call(f32[32,16,128]{2,1,0:T(8,128)S(1)} %all_to_all.15.all_ref), custom_call_target="tpu_custom_call" | custom-call | tf_op jit(solution)/shard_map/pallas_call | solution.py:549
  24.7 12.5 %all_to_all.16.image_ref = f32[32,8,128]{2,1,0:T(8,128)S(1)} all-to-all(f32[32,8,128]{2,1,0:T(8,128)S(1)} %get-tuple-element.16), channel_id=1, replica_groups=mesh['row'=4,'col'=8] {'row','col'}, dimensions={0} | all-to-all | bytes 262144 | tf_op jit(solution)/shard_map/all_to_all | solution.py:525
  37.1 2.3 %shard_map.61 = (f32[32,1,128]{2,1,0:T(1,128)S(1)}, f32[2,8,128]{2,1,0:T(8,128)S(1)}, f32[1,128]{1,0:T(1,128)S(1)}) custom-call(s32[1554]{0:T(1024)S(1)} %get-tuple-element.12.item_ref, s32[1]{0:T(128)} %get-tuple-element.13.count_ref, f32[20480,128]{1,0:T(8,128)S(1)} %get-tuple-element.14.coef_ref, f32[2,128]{1,0:T(2,128)S(1)} %get-tuple-element.15.kept_ref, ...), custom_call_target="tpu_custom_call" | custom-call | tf_op jit(solution)/shard_map/pallas_call | solution.py:570
  39.4 9.4 %all_to_all.17.line_ref = f32[32,1,128]{2,1,0:T(1,128)S(1)} all-to-all(f32[32,1,128]{2,1,0:T(1,128)S(1)} %get-tuple-element.19), channel_id=1, replica_groups=mesh['row'=4,'col'=8] {'row','col'}, dimensions={0} | all-to-all | bytes 32768 | tf_op jit(solution)/shard_map/all_to_all | solution.py:525
  48.8 0.0 copy-done
  48.8 0.8 %shard_map.62 = (f32[6,128]{1,0:T(8,128)}, f32[4]{0:T(128)}) custom-call(f32[6,128]{1,0:T(8,128)S(1)} %copy-done, f32[2,8,128]{2,1,0:T(8,128)S(1)} %get-tuple-element.17.pair_ref, f32[1,128]{1,0:T(1,128)S(1)} %get-tuple-element.18.scalar_ref, f32[32,1,128]{2,1,0:T(1,128)S(1)} %all_to_all.17.line_ref), custom_call_target="tpu_custom_call" | custom-call | tf_op jit(solution)/shard_map/pallas_call | solution.py:582
Async XLA Ops:
  0.6 48.2 %copy-start = (f32[6,128]{1,0:T(8,128)S(1)}, f32[6,128]{1,0:T(8,128)}, u32[]{:S(2)}) copy-start(f32[6,128]{1,0:T(8,128)} %config_ref.1) | copy-start | bytes 9220

commit v4 on v3

--- a/solution.py
+++ b/solution.py
@@ -21,7 +21,7 @@
 ITEM_MASK = 255
 LAYER = 16
 TESTS = 4
-GROUP = 2
+GROUP = 4
 TERMS = 20
 HELD = 128
 VMEM_LIMIT = 32 * 1024 * 1024

time: 49.7 us -> 49.8 us (level); the launches traced: 49.6 us -> 50.3 us
  Pallas kernels: 8.54 us -> 9.09 us
    pallas_call x1, Pallas kernels: 3.81 us -> 4.44 us  [local(): pl.pallas_call(functools.partial(first_kernel, row_devices, col_devices,...]
where the time goes in v4:
time: 49.8 us; the launch traced here: 50.3 us
  blocking collectives  39.9 us (80%)
  Pallas kernels  9.09 us (18%)
  between operations  1.32 us (3%)
    all_to_all x3, blocking collectives, everywhere(): return lax.all_to_all(copies, ('row', 'col'), 0, 0, tiled=True)  39.9 us
    pallas_call x1, Pallas kernels, local(): pl.pallas_call(functools.partial(first_kernel, row_devices, col_devices,...  4.44 us
    pallas_call x1, Pallas kernels, local(): pl.pallas_call(functools.partial(second_kernel, col_devices, total_entrie...  2.24 us
    pallas_call x1, Pallas kernels, local(): pl.pallas_call(pack_kernel, out_shape=shaped(devices, 2 * SUB, member), i...  1.61 us

profile of v4, /device:TPU:0, one launch (start us, length us, event | category | flops | bytes accessed | tf_op | source)
XLA Modules:
  0.0 50.3 jit_solution(4109468404457407095)
XLA Ops:
  0.6 0.0 copy-start
  1.3 1.6 %shard_map.59 = f32[32,16,128]{2,1,0:T(8,128)} custom-call(f32[6,128]{1,0:T(8,128)} %config_ref.1, f32[6,128]{1,0:T(8,128)} %refs_1_.1, s32[1,5,1,8]{3,2,1,0:T(1,128)} %bitcast.1, s32[1,1]{1,0:T(1,128)S(6)} %copy.6.refs_3_), custom_call_target="tpu_custom_call" | custom-call | tf_op jit(solution)/shard_map/pallas_call | solution.py:532
  2.9 17.9 %all_to_all.15.all_ref = f32[32,16,128]{2,1,0:T(8,128)S(1)} all-to-all(f32[32,16,128]{2,1,0:T(8,128)} %shard_map.59), channel_id=1, replica_groups=mesh['row'=4,'col'=8] {'row','col'}, dimensions={0} | all-to-all | bytes 524288 | tf_op jit(solution)/shard_map/all_to_all | solution.py:525
  20.8 4.4 %shard_map.60 = (f32[32,8,128]{2,1,0:T(8,128)S(1)}, s32[1556]{0:T(1024)S(1)}, s32[1]{0:T(128)}, f32[20480,128]{1,0:T(8,128)S(1)}, f32[2,128]{1,0:T(2,128)S(1)}) custom-call(f32[32,16,128]{2,1,0:T(8,128)S(1)} %all_to_all.15.all_ref), custom_call_target="tpu_custom_call" | custom-call | tf_op jit(solution)/shard_map/pallas_call | solution.py:549
  25.3 12.7 %all_to_all.16.image_ref = f32[32,8,128]{2,1,0:T(8,128)S(1)} all-to-all(f32[32,8,128]{2,1,0:T(8,128)S(1)} %get-tuple-element.16), channel_id=1, replica_groups=mesh['row'=4,'col'=8] {'row','col'}, dimensions={0} | all-to-all | bytes 262144 | tf_op jit(solution)/shard_map/all_to_all | solution.py:525
  38.0 2.2 %shard_map.61 = (f32[32,1,128]{2,1,0:T(1,128)S(1)}, f32[2,8,128]{2,1,0:T(8,128)S(1)}, f32[1,128]{1,0:T(1,128)S(1)}) custom-call(s32[1556]{0:T(1024)S(1)} %get-tuple-element.12.item_ref, s32[1]{0:T(128)} %get-tuple-element.13.count_ref, f32[20480,128]{1,0:T(8,128)S(1)} %get-tuple-element.14.coef_ref, f32[2,128]{1,0:T(2,128)S(1)} %get-tuple-element.15.kept_ref, ...), custom_call_target="tpu_custom_call" | custom-call | tf_op jit(solution)/shard_map/pallas_call | solution.py:570
  40.2 9.3 %all_to_all.17.line_ref = f32[32,1,128]{2,1,0:T(1,128)S(1)} all-to-all(f32[32,1,128]{2,1,0:T(1,128)S(1)} %get-tuple-element.19), channel_id=1, replica_groups=mesh['row'=4,'col'=8] {'row','col'}, dimensions={0} | all-to-all | bytes 32768 | tf_op jit(solution)/shard_map/all_to_all | solution.py:525
  49.5 0.0 copy-done
  49.5 0.8 %shard_map.62 = (f32[6,128]{1,0:T(8,128)}, f32[4]{0:T(128)}) custom-call(f32[6,128]{1,0:T(8,128)S(1)} %copy-done, f32[2,8,128]{2,1,0:T(8,128)S(1)} %get-tuple-element.17.pair_ref, f32[1,128]{1,0:T(1,128)S(1)} %get-tuple-element.18.scalar_ref, f32[32,1,128]{2,1,0:T(1,128)S(1)} %all_to_all.17.line_ref), custom_call_target="tpu_custom_call" | custom-call | tf_op jit(solution)/shard_map/pallas_call | solution.py:582
Async XLA Ops:
  0.6 48.9 %copy-start = (f32[6,128]{1,0:T(8,128)S(1)}, f32[6,128]{1,0:T(8,128)}, u32[]{:S(2)}) copy-start(f32[6,128]{1,0:T(8,128)} %config_ref.1) | copy-start | bytes 9220
